TPU v7x, 32 devices: a whole 2x2x4 slice. The times are simulated.
32 devices in a mesh: dp: 4 (over y, x), fsdp: 8 (over z, core).
Axes of the slice: x: 2, y: 2, z: 4, core: 2. Of those that a mesh axis runs over, the one named last changes fastest.
Arguments:
- states: bfloat16 [16384, 1024], P(('dp', 'fsdp')), may hold values from -6 to 6
- pad_mask: int32 [128, 128], P(('dp', 'fsdp')), may hold values from 0 to 1, as said below
- query_proj: bfloat16 [1024, 1024], P(('dp', 'fsdp')), may hold values from -0.1875 to 0.1875
- key_proj: bfloat16 [1024, 1024], P(('dp', 'fsdp')), may hold values from -0.1875 to 0.1875
- value_proj: bfloat16 [1024, 1024], P(('dp', 'fsdp')), may hold values from -0.1875 to 0.1875
- attn_proj: bfloat16 [1024, 1024], P(('dp', 'fsdp')), may hold values from -2 to 2
- query_bias: bfloat16 [1024], P(('dp', 'fsdp')), may hold values from -3 to 3
- value_bias: bfloat16 [1024], P(('dp', 'fsdp')), may hold values from -3 to 3
- attn_bias: bfloat16 [1024], P(('dp', 'fsdp')), may hold values from -3 to 3
- first_gain: bfloat16 [1024], P(('dp', 'fsdp')), may hold values from 0.5 to 1.5
- first_shift: bfloat16 [1024], P(('dp', 'fsdp')), may hold values from -3 to 3
- inner_proj: bfloat16 [1024, 4096], P(('dp', 'fsdp')), may hold values from -0.1875 to 0.1875
- inner_bias: bfloat16 [4096], P(('dp', 'fsdp')), may hold values from -3 to 3
- outer_proj: bfloat16 [4096, 1024], P(('dp', 'fsdp')), may hold values from -0.09375 to 0.09375
- outer_bias: bfloat16 [1024], P(('dp', 'fsdp')), may hold values from -3 to 3
- second_gain: bfloat16 [1024], P(('dp', 'fsdp')), may hold values from 0.5 to 1.5
- second_shift: bfloat16 [1024], P(('dp', 'fsdp')), may hold values from -3 to 3
- out_grad: bfloat16 [16384, 1024], P(('dp', 'fsdp')), may hold values from -6 to 6
Outputs:
- encoded: bfloat16 [16384, 1024], P(('dp', 'fsdp'))
- states_grad: float32 [16384, 1024], P(('dp', 'fsdp'))
- query_grad: float32 [1024, 1024], P(('dp', 'fsdp'))
- keys_grad: float32 [1024, 1024], P(('dp', 'fsdp'))
- values_grad: float32 [1024, 1024], P(('dp', 'fsdp'))
- attn_grad: float32 [1024, 1024], P(('dp', 'fsdp'))
- qbias_grad: float32 [1024], P(('dp', 'fsdp'))
- vbias_grad: float32 [1024], P(('dp', 'fsdp'))
- abias_grad: float32 [1024], P(('dp', 'fsdp'))
- fgain_grad: float32 [1024], P(('dp', 'fsdp'))
- fshift_grad: float32 [1024], P(('dp', 'fsdp'))
- inner_grad: float32 [1024, 4096], P(('dp', 'fsdp'))
- ibias_grad: float32 [4096], P(('dp', 'fsdp'))
- outer_grad: float32 [4096, 1024], P(('dp', 'fsdp'))
- obias_grad: float32 [1024], P(('dp', 'fsdp'))
- sgain_grad: float32 [1024], P(('dp', 'fsdp'))
- sshift_grad: float32 [1024], P(('dp', 'fsdp'))
Inputs may be any that keep to these rules, and one draw needn't show every extreme that they name: `pad_mask`: in each segment the ones form a prefix of 32 to 128 tokens.
All inputs are finite; a program needn't handle non-finite values.
Results may differ from a plain program's by a relative error of at most 0.014.
Values may be sent and summed in bfloat16 or wider, within the bound.
A program may use at most 256 MiB of HBM per device.

v0:
```python
import functools

import jax
import jax.numpy as jnp
from jax import lax
from jax.experimental import pallas as pl
from jax.experimental.pallas import tpu as pltpu
from jax.sharding import PartitionSpec as P

HEADS = 16
MESH = pl.DeviceIdType.MESH

epsilon = 1e-05
neg_fill = -1e30


class Place:
    def __init__(self, depth):
        dp = lax.axis_index("dp")
        fsdp = lax.axis_index("fsdp")
        self.depth = depth
        self.dp = dp
        self.z = fsdp // 2
        self.core = lax.rem(fsdp, 2)
        flip_x = dp + 1 - 2 * lax.rem(dp, 2)
        flip_y = lax.rem(dp + 2, 4)
        self.near = flip_x + self.core * (flip_y - flip_x)
        self.far = flip_y + self.core * (flip_x - flip_y)
        self.both = lax.rem(flip_x + 2, 4)
        self.fsdp = fsdp
        self.sibling = fsdp + 1 - 2 * self.core

    def up(self, step):
        return lax.rem(self.z + step, self.depth)

    def down(self, step):
        return lax.rem(self.z + self.depth - step, self.depth)

    def along(self, z):
        return (self.dp, z * 2 + self.core)

    def greet(self):
        barrier = pltpu.get_barrier_semaphore()
        others = [self.along(self.up(step)) for step in range(1, self.depth)]
        others += [(self.near, self.fsdp), (self.far, self.fsdp), (self.dp, self.sibling)]
        for other in others:
            pl.semaphore_signal(barrier, inc=1, device_id=other, device_id_type=MESH)
        pl.semaphore_wait(barrier, len(others))


def remote(source, target, send, recv, device):
    return pltpu.make_async_remote_copy(
        src_ref=source, dst_ref=target, send_sem=send, recv_sem=recv, device_id=device, device_id_type=MESH
    )


class Gather:
    def __init__(self, place, full, own, sems, piece):
        self.place, self.full, self.own, self.piece = place, full, own, piece
        self.su, self.ru, self.sd, self.rd, self.sb, self.rb, self.sa, self.ra, self.sc, self.rc, self.so = sems

    def copy_own(self):
        p = self.place
        return pltpu.make_async_copy(self.own, self.full.at[p.dp, p.z, p.core], self.so.at[self.piece])

    def copy_up(self, z, first=False):
        p = self.place
        block = self.full.at[p.dp, z, p.core]
        source = self.own if first else block
        return remote(source, block, self.su.at[self.piece, z], self.ru.at[self.piece, z], p.along(p.z + 1))

    def copy_down(self, z, first=False):
        p = self.place
        block = self.full.at[p.dp, z, p.core]
        source = self.own if first else block
        return remote(source, block, self.sd.at[self.piece, z], self.rd.at[self.piece, z], p.along(p.z - 1))

    def copy_near(self, z, first=False, arriving=False):
        p = self.place
        block = self.full.at[p.near if arriving else p.dp, z, p.core]
        source = self.own if first else block
        return remote(source, block, self.sb.at[self.piece, z], self.rb.at[self.piece, z], (p.near, p.fsdp))

    def copy_far(self, half, z, first=False, arriving=False):
        p = self.place
        row = (p.both if half else p.far) if arriving else (p.near if half else p.dp)
        block = self.full.at[row, z, p.core]
        source = self.own if first else block
        at = half * p.depth + z
        return remote(source, block, self.sa.at[self.piece, at], self.ra.at[self.piece, at], (p.far, p.fsdp))

    def copy_core(self, part, arriving=False):
        p = self.place
        if arriving:
            row = (p.dp, p.far, p.near, p.both)[part]
            block = self.full.at[row, :, 1 - p.core]
        else:
            row = (p.dp, p.near, p.far, p.both)[part]
            block = self.full.at[row, :, p.core]
        return remote(block, block, self.sc.at[self.piece, part], self.rc.at[self.piece, part], (p.dp, p.sibling))

    def start(self):
        p = self.place
        pl.when(p.z < p.depth - 1)(lambda: self.copy_up(p.z, True).start())
        pl.when(p.z > 0)(lambda: self.copy_down(p.z, True).start())
        self.copy_near(p.z, True).start()
        self.copy_far(0, p.z, True).start()
        self.copy_own().start()

    def hop(self, step):
        p = self.place

        @pl.when(p.z >= step)
        def _():
            z = p.z - step
            self.copy_up(z).wait_recv()
            pl.when(p.z < p.depth - 1)(lambda: self.copy_up(z).start())
            self.copy_near(z).start()
            self.copy_far(0, z).start()

        @pl.when(p.z + step < p.depth)
        def _():
            z = p.z + step
            self.copy_down(z).wait_recv()
            pl.when(p.z > 0)(lambda: self.copy_down(z).start())
            self.copy_near(z).start()
            self.copy_far(0, z).start()

    def last_hop(self):
        self.hop(self.place.depth - 1)
        self.copy_own().wait()
        self.copy_core(0).start()

    def spread(self, step):
        p = self.place

        def act(z):
            self.copy_near(z, arriving=True).wait_recv()
            self.copy_far(1, z).start()

        if step == 0:
            act(p.z)
        else:
            pl.when(p.z >= step)(lambda: act(p.z - step))
            pl.when(p.z + step < p.depth)(lambda: act(p.z + step))
        if step == p.depth - 1:
            self.copy_core(1).start()

    def arrive_far(self, half):
        p = self.place
        for z in range(p.depth):
            self.copy_far(half, z, arriving=True).wait_recv()
        self.copy_core(2 + half).start()

    def arrive_core(self, *parts):
        for part in parts:
            self.copy_core(part, arriving=True).wait_recv()

    def drain(self):
        p = self.place
        for z in range(p.depth):
            pl.when((p.z < p.depth - 1) & (z <= p.z))(lambda: self.copy_up(z).wait_send())
            pl.when((p.z > 0) & (z >= p.z))(lambda: self.copy_down(z).wait_send())
            self.copy_near(z).wait_send()
            self.copy_far(0, z).wait_send()
            self.copy_far(1, z).wait_send()
        for part in range(4):
            self.copy_core(part).wait_send()


def gather_sems(pieces, depth):
    dma = pltpu.SemaphoreType.DMA
    counts = (depth, depth, depth, depth, depth, depth, 2 * depth, 2 * depth, 4, 4)
    return [dma((pieces, count)) for count in counts] + [dma((pieces,))]


def matmul(left, right):
    return lax.dot_general(left, right, (((1,), (0,)), ((), ())), preferred_element_type=jnp.float32)


def matmul_nt(left, right):
    return lax.dot_general(left, right, (((1,), (1,)), ((), ())), preferred_element_type=jnp.float32)


def matmul_tn(left, right):
    return lax.dot_general(left, right, (((0,), (0,)), ((), ())), preferred_element_type=jnp.float32)


def flat(value):
    return value.reshape(-1, value.shape[-1])


def span(index, size):
    return pl.ds(pl.multiple_of(index * size, size), size)


def unpack_table(table, block, vectors):
    places = table.shape[0] * table.shape[1] * table.shape[2]
    width = vectors.shape[1]
    per_row = 128 // block
    lane = lax.broadcasted_iota(jnp.int32, (128, width), 1)
    source = lax.broadcasted_iota(jnp.int32, (128, width), 0)
    owner = lax.broadcasted_iota(jnp.int32, (places, width), 1) // block
    mine = owner == lax.broadcasted_iota(jnp.int32, (places, width), 0)
    for vector in range(8):
        row = table[:, :, :, vector // per_row, :].reshape(places, 128).astype(jnp.bfloat16)
        pick = jnp.where(source == lax.rem(lane, block) + block * (vector % per_row), 1.0, 0.0).astype(jnp.bfloat16)
        spread = jnp.where(mine, matmul(row, pick), 0.0)
        vectors[vector : vector + 1, :] = jnp.sum(spread, axis=0, keepdims=True)


def project(rows, weights, vectors, projected):
    width = rows.shape[1]
    for part, bias in ((0, 0), (1, None), (2, 1)):

        def one(index, _):
            at = span(index, 256)
            weight = flat(weights[:, :, :, :, part * width : (part + 1) * width])
            total = matmul(rows[at, :], weight)
            if bias is not None:
                total = total + vectors[bias : bias + 1, :]
            projected[at, part * width : (part + 1) * width] = total.astype(jnp.bfloat16)
            return 0

        lax.fori_loop(0, rows.shape[0] // 256, one, 0)


def head_lanes(heads, rows, size):
    lane = lax.broadcasted_iota(jnp.int32, (rows, heads * size), 1) // size
    return [lane == head for head in range(heads)]


def stack_heads(value, lanes):
    return jnp.concatenate([jnp.where(lane, value, jnp.zeros_like(value)) for lane in lanes], axis=0)


def merge_heads(value, lanes):
    rows = value.shape[0] // len(lanes)
    result = value[:rows]
    for head in range(1, len(lanes)):
        result = jnp.where(lanes[head], value[head * rows : (head + 1) * rows], result)
    return result


QUAD = 4


def attend(projected, keep, probs, context):
    width = context.shape[1]
    size = width // HEADS
    segments, length = keep.shape
    scale = size ** (-0.5)
    lanes = head_lanes(QUAD, length, size)
    quads = HEADS // QUAD

    def one(index, _):
        segment = index // quads
        quad = lax.rem(index, quads)
        at = span(segment, length)
        queries = projected[at, span(quad, QUAD * size)]
        keysets = projected[at, span(quad + quads, QUAD * size)]
        valuesets = projected[at, span(quad + 2 * quads, QUAD * size)]
        scores = matmul_nt(stack_heads(queries, lanes), keysets) * scale
        mask = keep[pl.ds(segment, 1), :] > 0
        scores = jnp.where(mask, scores, neg_fill)
        raised = jnp.exp(scores - jnp.max(scores, axis=1, keepdims=True))
        low = (raised / jnp.sum(raised, axis=1, keepdims=True)).astype(jnp.bfloat16)
        probs[index] = low
        context[at, span(quad, QUAD * size)] = merge_heads(matmul(low, valuesets), lanes).astype(jnp.bfloat16)
        return 0

    lax.fori_loop(0, segments * quads, one, 0)


def center_scale(hidden):
    center = hidden - jnp.mean(hidden, axis=1, keepdims=True)
    spread = jnp.mean(center * center, axis=1, keepdims=True)
    rate = lax.rsqrt(spread + epsilon)
    return center * rate, rate


def first_block(rows, context, weights, vectors, first_sum, first_norm, first_low):

    def one(index, _):
        at = span(index, 128)
        weight = flat(weights[...])
        total = rows[at, :].astype(jnp.float32) + (matmul(context[at, :], weight) + vectors[2:3, :])
        first_sum[at, :] = total
        normed, _ = center_scale(total)
        result = normed * vectors[3:4, :] + vectors[4:5, :]
        first_norm[at, :] = result
        first_low[at, :] = result.astype(jnp.bfloat16)
        return 0

    lax.fori_loop(0, rows.shape[0] // 128, one, 0)


def inner_block(first_low, weights, table, row_at, activated, slope):
    count = first_low.shape[0]
    biases = table.shape[0] * table.shape[1] * table.shape[2]
    chunks = weights.shape[4] // 512
    per_chunk = biases // chunks
    rows_of = table[:, :, :, row_at, :].reshape(biases, 128)
    for chunk in range(chunks):
        columns = slice(chunk * 512, (chunk + 1) * 512)
        first = chunk * per_chunk
        bias = jnp.concatenate([rows_of[first + part : first + part + 1] for part in range(per_chunk)], axis=1)

        def one(index, _):
            at = span(index, 128)
            value = matmul(first_low[at, :], flat(weights[:, :, :, :, columns])) + bias
            share = 0.5 * (1.0 + lax.erf(value * (0.5**0.5)))
            bell = jnp.exp(-0.5 * value * value) * ((0.5 / jnp.pi) ** 0.5)
            activated[at, columns] = (value * share).astype(jnp.bfloat16)
            slope[at, columns] = (share + value * bell).astype(jnp.bfloat16)
            return 0

        lax.fori_loop(0, count // 128, one, 0)


def outer_part(activated, weights, row, total, fresh):
    size = weights.shape[1] * weights.shape[2] * weights.shape[3]

    def one(index, _):
        at = span(index, 256)
        value = matmul(activated[at, span(row, size)], flat(weights[row]))
        total[at, :] = value if fresh else total[at, :] + value
        return 0

    lax.fori_loop(0, activated.shape[0] // 256, one, 0)


def norm_back(grad, normed, rate, gain):
    scaled = grad * gain
    mean = jnp.mean(scaled, axis=1, keepdims=True)
    along = jnp.mean(scaled * normed, axis=1, keepdims=True)
    return rate * (scaled - mean - normed * along)


def second_block(first_norm, total, cotangent, vectors, encoded, second_grad, outer_low, sums):
    sums[...] = jnp.zeros_like(sums)

    def one(index, _):
        at = span(index, 128)
        normed, rate = center_scale(first_norm[at, :] + (total[at, :] + vectors[5:6, :]))
        gain = vectors[6:7, :]
        encoded[at, :] = (normed * gain + vectors[7:8, :]).astype(jnp.bfloat16)
        grad = cotangent[at, :].astype(jnp.float32)
        back = norm_back(grad, normed, rate, gain)
        low = back.astype(jnp.bfloat16)
        second_grad[at, :] = back
        outer_low[at, :] = low
        sums[5:6, :] += jnp.sum(low.astype(jnp.float32), axis=0, keepdims=True)
        sums[6:7, :] += jnp.sum(grad * normed, axis=0, keepdims=True)
        sums[7:8, :] += jnp.sum(grad, axis=0, keepdims=True)
        return 0

    lax.fori_loop(0, first_norm.shape[0] // 128, one, 0)


def forward_kernel(depth, block, *refs):
    (rows, keep, cotangent, query_own, key_own, value_own, attn_own, inner_own, outer_own, table_own) = refs[:10]
    merged_out, attn_out, inner_out, outer_out = refs[10:14]
    (encoded_out, projected_out, probs_out, context_out, first_sum_out, first_low_out, activated_out, slope_out,
     second_grad_out, outer_low_out, vectors, sums) = refs[14:26]
    (merged_own, table, merged, attn, inner, outer, projected, probs, context, first_sum, first_norm, first_low, activated,
     slope, total, encoded, second_grad, outer_low, save_sem) = refs[26:45]
    sems = refs[45:]
    place = Place(depth)
    width = rows.shape[1]
    for part, own in enumerate((query_own, key_own, value_own)):
        merged_own[:, part * width : (part + 1) * width] = own[...]
    net_table = Gather(place, table, table_own, sems, 0)
    net_merged = Gather(place, merged, merged_own, sems, 1)
    net_attn = Gather(place, attn, attn_own, sems, 2)
    net_inner = Gather(place, inner, inner_own, sems, 3)
    net_outer = Gather(place, outer, outer_own, sems, 4)
    nets = (net_table, net_merged, net_attn, net_inner, net_outer)
    front = nets[:3]
    place.greet()
    saves = []

    def save(source, target):
        copy = pltpu.make_async_copy(source, target, save_sem.at[len(saves)])
        copy.start()
        saves.append(copy)

    def hop(net, step):
        if step == depth - 1:
            net.last_hop()
        else:
            net.hop(step)

    for net in front:
        net.start()
    for step in range(1, depth):
        for net in front:
            hop(net, step)
        if step == 1:
            net_inner.start()
        for net in front:
            net.spread(step - 1)
    for net in front:
        net.spread(depth - 1)
    hop(net_inner, 1)
    net_inner.spread(0)
    net_outer.start()
    for net in front:
        net.arrive_far(0)
        net.arrive_far(1)
        net.arrive_core(0, 1, 2, 3)
    save(merged, merged_out)
    save(attn, attn_out)
    unpack_table(table, block, vectors)
    project(rows, merged, vectors, projected)
    save(projected, projected_out)
    for step in range(2, depth):
        hop(net_inner, step)
        net_inner.spread(step - 1)
    net_inner.spread(depth - 1)
    attend(projected, keep, probs, context)
    save(probs, probs_out)
    save(context, context_out)
    hop(net_outer, 1)
    net_outer.spread(0)
    first_block(rows, context, attn, vectors, first_sum, first_norm, first_low)
    save(first_sum, first_sum_out)
    save(first_low, first_low_out)
    for step in range(2, depth):
        hop(net_outer, step)
        net_outer.spread(step - 1)
    net_outer.spread(depth - 1)
    net_inner.arrive_far(0)
    net_inner.arrive_far(1)
    net_inner.arrive_core(0, 1, 2, 3)
    save(inner, inner_out)
    inner_block(first_low, inner, table, 8 * block // 128, activated, slope)
    save(activated, activated_out)
    save(slope, slope_out)
    net_outer.arrive_core(0)
    outer_part(activated, outer, place.dp, total, True)
    net_outer.arrive_far(0)
    net_outer.arrive_core(1, 2)
    outer_part(activated, outer, place.near, total, False)
    outer_part(activated, outer, place.far, total, False)
    net_outer.arrive_far(1)
    net_outer.arrive_core(3)
    save(outer, outer_out)
    outer_part(activated, outer, place.both, total, False)
    second_block(first_norm, total, cotangent, vectors, encoded, second_grad, outer_low, sums)
    save(encoded, encoded_out)
    save(second_grad, second_grad_out)
    save(outer_low, outer_low_out)
    for net in nets:
        net.drain()
    for copy in saves:
        copy.wait()


def forward_all(depth, block, rows, keep, cotangent, owns):
    query_own, _, _, attn_own, inner_own, outer_own, table_own = owns
    tokens, width = rows.shape
    hidden = inner_own.shape[1]
    segments, length = keep.shape
    low, high = jnp.bfloat16, jnp.float32

    def fulls(own, columns):
        return (4, depth, 2, own.shape[0], columns)

    full_shapes = [fulls(query_own, 3 * width), fulls(attn_own, width), fulls(inner_own, hidden), fulls(outer_own, width)]
    kept = [
        ((tokens, width), low),
        ((tokens, 3 * width), low),
        ((segments * HEADS // QUAD, QUAD * length, length), low),
        ((tokens, width), low),
        ((tokens, width), high),
        ((tokens, width), low),
        ((tokens, hidden), low),
        ((tokens, hidden), low),
        ((tokens, width), high),
        ((tokens, width), low),
    ]
    small = [((8, width), high), ((8, width), high)]
    shapes = [jax.ShapeDtypeStruct(shape, low) for shape in full_shapes]
    shapes += [jax.ShapeDtypeStruct(*one) for one in kept + small]
    held = {name: pltpu.VMEM(*one) for name, one in zip(
        ("encoded", "projected", "probs", "context", "first_sum", "first_low", "activated", "slope", "second_grad", "outer_low"),
        kept)}
    scratch = [pltpu.VMEM((query_own.shape[0], 3 * width), low), pltpu.VMEM(fulls(table_own, 128), high)]
    scratch += [pltpu.VMEM(shape, low) for shape in full_shapes]
    scratch += [held[name] for name in ("projected", "probs", "context", "first_sum")]
    scratch += [pltpu.VMEM((tokens, width), high)]
    scratch += [held[name] for name in ("first_low", "activated", "slope")]
    scratch += [pltpu.VMEM((tokens, width), high)]
    scratch += [held[name] for name in ("encoded", "second_grad", "outer_low")]
    scratch += [pltpu.SemaphoreType.DMA((len(full_shapes) + len(kept),))]
    here = pl.BlockSpec(memory_space=pltpu.VMEM)
    away = pl.BlockSpec(memory_space=pl.ANY)
    return pl.pallas_call(
        functools.partial(forward_kernel, depth, block),
        out_shape=shapes,
        in_specs=[here] * 10,
        out_specs=[away] * (len(full_shapes) + len(kept)) + [here] * 2,
        scratch_shapes=scratch + gather_sems(5, depth),
        compiler_params=pltpu.CompilerParams(
            collective_id=0, has_side_effects=True, vmem_limit_bytes=60 * 1024 * 1024
        ),
        name="forward",
    )(rows, keep, cotangent, *owns)


SUBS = 4


class Slots:
    def __init__(self, core, far, near, along):
        self.core, self.far, self.near, self.along = core, far, near, along


class Scatter:
    def __init__(self, place, whole, slots, sems, credits, number, lot, first, count, after=False, before=False,
                 late_after=False, late_before=False):
        self.place, self.whole, self.slots = place, whole, slots
        self.sc, self.rc, self.sa, self.ra, self.sb, self.rb, self.sz, self.rz = sems
        self.core_free, self.far_free, self.near_free, self.z_free = credits
        self.number, self.lot, self.first, self.count = number, lot, first, count
        self.sub = first // count
        self.after, self.before, self.late_after, self.late_before = after, before, late_after, late_before
        self.tile = 8 if whole.dtype == jnp.float32 else 16

    def lines(self):
        return pl.ds(self.first, self.count)

    def mine(self, row):
        return self.whole.at[row, :, self.place.core, self.lines()]

    def sent_row(self, at):
        p = self.place
        return (p.both, p.near, p.far, p.dp)[at]

    def got_row(self, at):
        p = self.place
        return (p.both, p.far, p.near, p.dp)[at]

    def copy_core(self, at):
        p = self.place
        return remote(
            self.whole.at[self.sent_row(at), :, 1 - p.core, self.lines()], self.slots.core.at[at, :, self.lines()],
            self.sc.at[self.number, at], self.rc.at[self.number, at], (p.dp, p.sibling),
        )

    def copy_far(self, half):
        p = self.place
        return remote(
            self.mine(p.both if half else p.far), self.slots.far.at[self.lot, half, :, self.lines()],
            self.sa.at[self.number, half], self.ra.at[self.number, half], (p.far, p.fsdp),
        )

    def copy_near(self):
        p = self.place
        return remote(
            self.mine(p.near), self.slots.near.at[self.lot, :, self.lines()], self.sb.at[self.number],
            self.rb.at[self.number], (p.near, p.fsdp),
        )

    def copy_z(self, step):
        p = self.place
        return remote(
            self.whole.at[p.dp, p.up(step), p.core, self.lines()], self.slots.along.at[self.lot, step - 1, self.lines()],
            self.sz.at[self.number, step - 1], self.rz.at[self.number, step - 1], p.along(p.up(step)),
        )

    def add(self, row, slot):
        p = self.place
        tiles = self.count // self.tile

        def one(index, _):
            z = index // tiles
            at = pl.ds(pl.multiple_of(self.first + lax.rem(index, tiles) * self.tile, self.tile), self.tile)
            self.whole[row, z, p.core, at, :] = self.whole[row, z, p.core, at, :] + slot[z, at, :]
            return 0

        lax.fori_loop(0, p.depth * tiles, one, 0)

    def start_core(self, at):
        if self.after:
            pl.semaphore_wait(self.core_free.at[at, self.sub], 1)
        self.copy_core(at).start()

    def add_core(self, at):
        p = self.place
        self.copy_core(at).wait_recv()
        self.add(self.got_row(at), self.slots.core.at[at])
        if self.before:
            pl.semaphore_signal(self.core_free.at[at, self.sub], inc=1, device_id=(p.dp, p.sibling), device_id_type=MESH)
        if at < 2:
            if self.late_after:
                pl.semaphore_wait(self.far_free.at[1 - at, self.sub], 1)
            self.copy_far(1 - at).start()

    def add_far(self, half):
        p = self.place
        self.copy_far(half).wait_recv()
        self.add(p.near if half else p.dp, self.slots.far.at[self.lot, half])
        if self.late_before:
            pl.semaphore_signal(self.far_free.at[half, self.sub], inc=1, device_id=(p.far, p.fsdp), device_id_type=MESH)
        if half:
            if self.late_after:
                pl.semaphore_wait(self.near_free.at[self.sub], 1)
            self.copy_near().start()

    def add_near(self):
        p = self.place
        self.copy_near().wait_recv()
        self.add(p.dp, self.slots.near.at[self.lot])
        if self.late_before:
            pl.semaphore_signal(self.near_free.at[self.sub], inc=1, device_id=(p.near, p.fsdp), device_id_type=MESH)
        for step in range(1, p.depth):
            if self.late_after:
                pl.semaphore_wait(self.z_free.at[self.sub, step - 1], 1)
            self.copy_z(step).start()

    def finish(self, out):
        p = self.place
        for step in range(1, p.depth):
            self.copy_z(step).wait_recv()

        def one(index, _):
            start = pl.multiple_of(index * self.tile, self.tile)
            at = pl.ds(pl.multiple_of(self.first + start, self.tile), self.tile)
            total = self.whole[p.dp, p.z, p.core, at, :].astype(jnp.float32)
            for step in range(p.depth - 1):
                total = total + self.slots.along[self.lot, step, at, :].astype(jnp.float32)
            out[pl.ds(start, self.tile), :] = total
            return 0

        lax.fori_loop(0, self.count // self.tile, one, 0)
        if self.late_before:
            for step in range(1, p.depth):
                pl.semaphore_signal(
                    self.z_free.at[self.sub, step - 1], inc=1, device_id=p.along(p.down(step)), device_id_type=MESH
                )

    def drain(self):
        for at in range(4):
            self.copy_core(at).wait_send()
        self.copy_far(1).wait_send()
        self.copy_far(0).wait_send()
        self.copy_near().wait_send()
        for step in range(1, self.place.depth):
            self.copy_z(step).wait_send()


def outer_gradient(acts, low, grads, row):
    depth, cores, count, _ = grads.shape[1:]
    size = cores * count

    def one(z, _):
        value = matmul_tn(acts[row, :, span(z, size)], low[...])
        grads[row, z] = value.astype(jnp.bfloat16).reshape(grads.shape[2:])
        return 0

    lax.fori_loop(0, depth, one, 0)


def input_gradient(inputs, low, grads, row, part):
    depth, cores, count, width = grads.shape[1:]
    size = inputs.shape[1] // grads.shape[0]
    lines = count // SUBS
    value = matmul_tn(inputs[:, span(row, size)], low)
    grads[row, :, :, part * lines : (part + 1) * lines, :] = value.astype(jnp.bfloat16).reshape(depth, cores, lines, width)


def hidden_back(low, weights, slopes, bias_sum):
    width = low.shape[1]
    for part in range(SUBS):
        bias_sum[:, part * width : (part + 1) * width] = jnp.zeros((1, width), jnp.float32)

        def one(index, _):
            at = span(index, 128)
            value = matmul_nt(low[at, :], flat(weights[part])) * slopes[SUBS + part, at, :].astype(jnp.float32)
            rounded = value.astype(jnp.bfloat16)
            slopes[SUBS + part, at, :] = rounded
            bias_sum[:, part * width : (part + 1) * width] += jnp.sum(rounded.astype(jnp.float32), axis=0, keepdims=True)
            return 0

        lax.fori_loop(0, low.shape[0] // 128, one, 0)


def first_total_part(grad, inner_low, weights, part):
    lines = weights.shape[3] // SUBS

    def one(index, _):
        at = span(index, 128)
        weight = flat(weights[:, :, :, part * lines : (part + 1) * lines, :])
        grad[at, :] += matmul_nt(inner_low[SUBS + part, at, :], weight)
        return 0

    lax.fori_loop(0, grad.shape[0] // 128, one, 0)


def first_back(first_sum, grad, low, vectors, sums):
    for row in (2, 3, 4):
        sums[row : row + 1, :] = jnp.zeros((1, grad.shape[1]), jnp.float32)

    def one(index, _):
        at = span(index, 64)
        normed, rate = center_scale(first_sum[at, :])
        upper = grad[at, :]
        back = norm_back(upper, normed, rate, vectors[3:4, :])
        rounded = back.astype(jnp.bfloat16)
        grad[at, :] = back
        low[at, :] = rounded
        sums[2:3, :] += jnp.sum(rounded.astype(jnp.float32), axis=0, keepdims=True)
        sums[3:4, :] += jnp.sum(upper * normed, axis=0, keepdims=True)
        sums[4:5, :] += jnp.sum(upper, axis=0, keepdims=True)
        return 0

    lax.fori_loop(0, grad.shape[0] // 64, one, 0)


def context_back(low, weights, context):
    def one(index, _):
        at = span(index, 128)
        context[at, :] = matmul_nt(low[at, :], flat(weights[0:2])).astype(jnp.bfloat16)
        return 0

    lax.fori_loop(0, low.shape[0] // 128, one, 0)


def attend_back(projected, probs, context_low, sums, first, last):
    width = context_low.shape[1]
    size = width // HEADS
    length = probs.shape[2]
    scale = size ** (-0.5)
    lanes = head_lanes(QUAD, length, size)
    quads = HEADS // QUAD

    def one(index, _):
        segment = index // quads
        quad = lax.rem(index, quads)
        at = span(segment, length)
        columns = [span(quad + part * quads, QUAD * size) for part in range(3)]
        queries, keysets, valuesets = [projected[at, column] for column in columns]
        low = probs[index]
        wide = low.astype(jnp.float32)
        upper = stack_heads(context_low[at, columns[0]], lanes)
        prob_grad = matmul_nt(upper, valuesets)
        score_low = (wide * (prob_grad - jnp.sum(wide * prob_grad, axis=1, keepdims=True))).astype(jnp.bfloat16)
        value_low = matmul_tn(low, upper).astype(jnp.bfloat16)
        query_low = (merge_heads(matmul(score_low, keysets), lanes) * scale).astype(jnp.bfloat16)
        key_low = (matmul_tn(score_low, stack_heads(queries, lanes)) * scale).astype(jnp.bfloat16)
        projected[at, columns[0]] = query_low
        projected[at, columns[1]] = key_low
        projected[at, columns[2]] = value_low
        sums[0:1, columns[0]] += jnp.sum(query_low.astype(jnp.float32), axis=0, keepdims=True)
        sums[1:2, columns[0]] += jnp.sum(value_low.astype(jnp.float32), axis=0, keepdims=True)
        return 0

    lax.fori_loop(first, last, one, 0)


def states_back(grad, projected, weights):
    width = grad.shape[1]

    def one(index, _):
        at = span(index, 128)
        total = grad[at, :]
        for part in range(3):
            weight = flat(weights[2 + 2 * part : 4 + 2 * part])
            total = total + matmul_nt(projected[at, part * width : (part + 1) * width], weight)
        grad[at, :] = total
        return 0

    lax.fori_loop(0, grad.shape[0] // 128, one, 0)


def pack_sums(sums, bias_sum, block, table):
    dps, depth, cores = table.shape[:3]
    places = dps * depth * cores
    width = sums.shape[1]
    per_row = 128 // block
    lane = lax.broadcasted_iota(jnp.int32, (width, 128), 1)
    source = lax.broadcasted_iota(jnp.int32, (width, 128), 0)
    owner = lax.broadcasted_iota(jnp.int32, (places, width), 1) // block
    mine = owner == lax.broadcasted_iota(jnp.int32, (places, width), 0)
    table[...] = jnp.zeros_like(table)
    for row in range(8 // per_row):
        total = jnp.zeros((places, 128), jnp.float32)
        for part in range(per_row):
            vector = row * per_row + part
            pick = jnp.where(lane == lax.rem(source, block) + block * part, 1.0, 0.0).astype(jnp.bfloat16)
            value = jnp.where(mine, sums[vector : vector + 1, :], 0.0)
            upper = value.astype(jnp.bfloat16)
            lower = (value - upper.astype(jnp.float32)).astype(jnp.bfloat16)
            both = matmul(jnp.concatenate((upper, lower), axis=0), pick)
            total = total + (both[:places] + both[places:])
        table[:, :, :, row, :] = total.reshape(dps, depth, cores, 128)
    row = 8 * block // 128
    for index in range(places):
        dp, z, core = index // (depth * cores), index // cores % depth, index % cores
        table[dp, z, core, row : row + 1, :] = bias_sum[:, index * 128 : (index + 1) * 128]


def backward_kernel(depth, block, *refs):
    (vectors, known, rows_in, activated_in, slope_in, outer_low_in, second_grad_in, first_sum_in, first_low_in, context_in,
     projected_in, probs_in, merged_in, attn_in, inner_in, outer_in) = refs[:16]
    states_out, outer_out, inner_out, query_out, key_out, value_out, attn_out, table_out = refs[16:24]
    (first_buffer, second_buffer, outer_grads, wide, from_core, from_far, from_near, from_z, low, first_low, grad, first_sum,
     context, projected, probs, rows, sums, bias_sum, table, table_core, table_far, table_near, table_z) = refs[24:47]
    load_sem, save_sem = refs[47:49]
    sems = refs[49:57]
    credits = refs[57:61]
    place = Place(depth)
    width = rows.shape[1]
    tokens = rows.shape[0]
    lines = outer_grads.shape[3] // SUBS
    loads = []

    def load(source, target):
        copy = pltpu.make_async_copy(source, target, load_sem.at[len(loads)])
        copy.start()
        loads.append(copy)
        return copy

    def load_columns(source, targets):
        return [load(source.at[:, part * width : (part + 1) * width], target) for part, target in enumerate(targets)]

    low_load = load(outer_low_in, low)
    act_loads = load_columns(activated_in, [wide.at[part] for part in range(SUBS)])
    outer_load = load(outer_in, first_buffer)
    slope_loads = load_columns(slope_in, [wide.at[SUBS + part] for part in range(SUBS)])
    first_low_load = load(first_low_in, first_low)
    grad_load = load(second_grad_in, grad)
    inner_loads = [
        load(inner_in.at[:, :, :, :, part * width : (part + 1) * width],
             second_buffer.at[:, :, :, part * lines : (part + 1) * lines, :])
        for part in range(SUBS)
    ]
    first_sum_load = load(first_sum_in, first_sum)
    context_load = load(context_in, context)
    projected_load = load(projected_in, projected)
    probs_load = load(probs_in, probs)
    rows_load = load(rows_in, rows)

    slots = Slots(from_core, from_far, from_near, from_z)
    table_slots = Slots(table_core, table_far, table_near, table_z)
    outers = [
        Scatter(place, outer_grads, slots, sems, credits, sub, 0, sub * lines, lines, before=True, late_before=True)
        for sub in range(SUBS)
    ]
    inner_grads = first_buffer
    inners = [
        Scatter(place, inner_grads, slots, sems, credits, SUBS + sub, 1, sub * lines, lines, after=True, before=True)
        for sub in range(SUBS)
    ]
    other_grads = second_buffer
    others = [
        Scatter(place, other_grads, slots, sems, credits, 2 * SUBS + sub, 0, sub * lines, lines, after=True, late_after=True)
        for sub in range(SUBS)
    ]
    attn_net = others[3]
    mergeds = others[:3]
    small = Scatter(place, table, table_slots, sems, credits, 3 * SUBS, 0, 0, 8)
    row_order = (place.both, place.near, place.far, place.dp)
    sums[...] = known[...]
    sums[0:2, :] = jnp.zeros((2, width), jnp.float32)
    place.greet()

    def pieces(nets, compute):
        for at in range(4):
            compute(row_order[at])
            for net in nets:
                net.start_core(at)
            if at:
                for net in nets:
                    net.add_core(at - 1)
        for net in nets:
            net.add_core(3)

    low_load.wait()
    for copy in act_loads:
        copy.wait()
    pieces(outers, lambda row: outer_gradient(wide, low, outer_grads, row))
    half = tokens
    attn_loads = [load(attn_in.at[part * half : (part + 1) * half], wide.at[part]) for part in range(2)]

    def load_merged(part):
        return [
            load(merged_in.at[at * half : (at + 1) * half, part * width : (part + 1) * width], wide.at[2 + 2 * part + at])
            for at in range(2)
        ]

    merged_loads = load_merged(0)
    outer_load.wait()
    for copy in slope_loads:
        copy.wait()
    hidden_back(low, first_buffer, wide, bias_sum)
    first_low_load.wait()

    def inner_rows(row):
        for part in range(SUBS):
            input_gradient(first_low, wide[SUBS + part], inner_grads, row, part)

    pieces(inners, inner_rows)
    for net in outers:
        net.add_far(1)
    grad_load.wait()
    for copy in inner_loads:
        copy.wait()
    for part in range(SUBS):
        first_total_part(grad, wide, second_buffer, part)
    merged_loads += load_merged(1) + load_merged(2)
    for net in outers:
        net.add_far(0)
    first_sum_load.wait()
    first_back(first_sum, grad, low, vectors, sums)
    context_load.wait()
    pieces([attn_net], lambda row: input_gradient(context, low[...], other_grads, row, 3))
    for copy in attn_loads:
        copy.wait()
    context_back(low, wide, context)
    for net in outers:
        net.add_near()
    projected_load.wait()
    probs_load.wait()
    count = probs.shape[0]
    attend_back(projected, probs, context, sums, 0, count // 2)
    for net in inners:
        net.add_far(1)
    attend_back(projected, probs, context, sums, count // 2, count)
    rows_load.wait()

    def merged_rows(row):
        for part in range(3):
            input_gradient(rows, projected[:, part * width : (part + 1) * width], other_grads, row, part)

    for sub, net in enumerate(outers):
        net.finish(outer_out.at[pl.ds(sub * lines, lines), :])
    pieces(mergeds, merged_rows)
    for net in inners:
        net.add_far(0)
    pack_sums(sums, bias_sum, block, table)
    pieces([small], lambda row: None)
    for copy in merged_loads:
        copy.wait()
    states_back(grad, projected, wide)
    save = pltpu.make_async_copy(grad, states_out, save_sem)
    save.start()
    for net in inners:
        net.add_near()
    last = [attn_net] + mergeds + [small]
    for net in last:
        net.add_far(1)
    for net in last:
        net.add_far(0)
        net.add_near()
    for sub, net in enumerate(inners):
        net.finish(inner_out.at[:, pl.ds(sub * width, width)])
    for net, out in zip(last, (attn_out, query_out, key_out, value_out, table_out)):
        net.finish(out)
    for net in outers + inners + last:
        net.drain()
    save.wait()


def backward_all(depth, block, vectors, known, kept):
    low, high = jnp.bfloat16, jnp.float32
    (rows, activated, _, _, _, first_sum, _, _, projected, probs, _, _, inner, outer) = kept
    tokens, width = rows.shape
    hidden = activated.shape[1]
    unit = outer.shape
    lines = unit[3]
    own_rows = lines // SUBS
    dma, regular = pltpu.SemaphoreType.DMA, pltpu.SemaphoreType.REGULAR
    nets = 3 * SUBS + 1
    scratch = [
        pltpu.VMEM(unit, low),
        pltpu.VMEM(unit, low),
        pltpu.VMEM(unit, low),
        pltpu.VMEM((2 * SUBS, tokens, width), low),
        pltpu.VMEM((4, depth, lines, width), low),
        pltpu.VMEM((2, 2, depth, lines, width), low),
        pltpu.VMEM((2, depth, lines, width), low),
        pltpu.VMEM((2, depth - 1, lines, width), low),
        pltpu.VMEM((tokens, width), low),
        pltpu.VMEM((tokens, width), low),
        pltpu.VMEM((tokens, width), high),
        pltpu.VMEM((tokens, width), high),
        pltpu.VMEM((tokens, width), low),
        pltpu.VMEM(projected.shape, low),
        pltpu.VMEM(probs.shape, low),
        pltpu.VMEM((tokens, width), low),
        pltpu.VMEM((8, width), high),
        pltpu.VMEM((1, hidden), high),
        pltpu.VMEM((4, depth, 2, 8, 128), high),
        pltpu.VMEM((4, depth, 8, 128), high),
        pltpu.VMEM((1, 2, depth, 8, 128), high),
        pltpu.VMEM((1, depth, 8, 128), high),
        pltpu.VMEM((1, depth - 1, 8, 128), high),
        dma((40,)),
        dma,
        dma((nets, 4)), dma((nets, 4)), dma((nets, 2)), dma((nets, 2)), dma((nets,)), dma((nets,)),
        dma((nets, depth - 1)), dma((nets, depth - 1)),
        regular((4, SUBS)), regular((2, SUBS)), regular((SUBS,)), regular((SUBS, depth - 1)),
    ]
    shapes = [(tokens, width), (lines, width), (own_rows, hidden)] + [(own_rows, width)] * 4 + [(8, 128)]
    here = pl.BlockSpec(memory_space=pltpu.VMEM)
    away = pl.BlockSpec(memory_space=pl.ANY)
    return pl.pallas_call(
        functools.partial(backward_kernel, depth, block),
        out_shape=[jax.ShapeDtypeStruct(shape, high) for shape in shapes],
        in_specs=[here] * 2 + [away] * len(kept),
        out_specs=[away] + [here] * 7,
        scratch_shapes=scratch,
        compiler_params=pltpu.CompilerParams(
            collective_id=1, has_side_effects=True, vmem_limit_bytes=62 * 1024 * 1024
        ),
        name="backward",
    )(vectors, known, *kept)


def normalize(hidden, gain, shift):
    center = hidden - jnp.mean(hidden, axis=-1, keepdims=True)
    spread = jnp.mean(center * center, axis=-1, keepdims=True)
    return center * lax.rsqrt(spread + epsilon) * gain + shift


def exact_gelu(value):
    return jax.nn.gelu(value, approximate=False)


def contract_rows(left, right):
    return lax.dot_general(
        left, right, (((0,), (0,)), ((), ())), preferred_element_type=jnp.float32
    )


def times_transposed(left, right):
    return lax.dot_general(
        left, right, (((1,), (1,)), ((), ())), preferred_element_type=jnp.float32
    )


def collect(merged, attn, inner, outer, vectors, widened):
    return (
        lax.all_gather(merged, ("dp", "fsdp"), axis=0, tiled=True),
        lax.all_gather(attn, ("dp", "fsdp"), axis=0, tiled=True),
        lax.all_gather(inner, ("dp", "fsdp"), axis=0, tiled=True),
        lax.all_gather(outer, ("dp", "fsdp"), axis=0, tiled=True),
        lax.all_gather(vectors, ("dp", "fsdp"), axis=0, tiled=True),
        lax.all_gather(widened, ("dp", "fsdp"), axis=0, tiled=True),
    )


def reduce_grads(merged, attn, inner, outer, vectors, widened):
    return (
        lax.psum_scatter(merged, ("dp", "fsdp"), scatter_dimension=0, tiled=True),
        lax.psum_scatter(attn, ("dp", "fsdp"), scatter_dimension=0, tiled=True),
        lax.psum_scatter(inner, ("dp", "fsdp"), scatter_dimension=0, tiled=True),
        lax.psum_scatter(outer, ("dp", "fsdp"), scatter_dimension=0, tiled=True),
        lax.psum_scatter(vectors, ("dp", "fsdp"), scatter_dimension=0, tiled=True),
        lax.psum_scatter(widened, ("dp", "fsdp"), scatter_dimension=0, tiled=True),
    )


def split_heads(projected, segments):
    total_rows, triple = projected.shape
    width = triple // 3
    return projected.reshape(segments, total_rows // segments, 3, HEADS, width // HEADS)


def attention_probs(queries, keysets, keep, scale):
    scores = (
        jnp.einsum("sqhd,skhd->shqk", queries, keysets, preferred_element_type=jnp.float32) * scale
    )
    scores = jnp.where(keep[:, None, None, :] > 0, scores, neg_fill)
    peaks = jnp.max(scores, axis=-1, keepdims=True)
    raised = jnp.exp(scores - peaks)
    return raised / jnp.sum(raised, axis=-1, keepdims=True)


def forward_pass(rows, keep, weights):
    merged, attn, inner, outer, vectors, widened = weights
    vector_full = vectors.astype(jnp.float32)
    width = rows.shape[1]
    scale = (width // HEADS) ** (-0.5)
    merged_bias = jnp.concatenate(
        (vector_full[:, 0], jnp.zeros((width,), jnp.float32), vector_full[:, 1])
    )
    projected = (jnp.dot(rows, merged, preferred_element_type=jnp.float32) + merged_bias).astype(
        jnp.bfloat16
    )
    split = split_heads(projected, keep.shape[0])
    probs = attention_probs(split[:, :, 0], split[:, :, 1], keep, scale).astype(jnp.bfloat16)
    context = jnp.einsum(
        "shqk,skhd->sqhd", probs, split[:, :, 2], preferred_element_type=jnp.float32
    )
    context = context.reshape(rows.shape[0], width).astype(jnp.bfloat16)
    attended = jnp.dot(context, attn, preferred_element_type=jnp.float32) + vector_full[:, 2]
    first_sum = rows.astype(jnp.float32) + attended
    first_norm = normalize(first_sum, vector_full[:, 3], vector_full[:, 4])
    first_low = first_norm.astype(jnp.bfloat16)
    inner_act = jnp.dot(first_low, inner, preferred_element_type=jnp.float32) + widened.astype(
        jnp.float32
    )
    activated = exact_gelu(inner_act).astype(jnp.bfloat16)
    outer_act = jnp.dot(activated, outer, preferred_element_type=jnp.float32) + vector_full[:, 5]
    second_sum = first_norm + outer_act
    encoded = normalize(second_sum, vector_full[:, 6], vector_full[:, 7]).astype(jnp.bfloat16)
    return (encoded, (projected, context, first_sum, first_low, inner_act, activated, second_sum))


def backward_pass(rows, keep, cotangent, weights, kept):
    merged, attn, inner, outer, vectors, widened = weights
    projected, context, first_sum, first_low, inner_act, activated, second_sum = kept
    vector_full = vectors.astype(jnp.float32)
    width = rows.shape[1]
    scale = (width // HEADS) ** (-0.5)
    second_out, second_pull = jax.vjp(normalize, second_sum, vector_full[:, 6], vector_full[:, 7])
    second_grad, second_gain_g, second_shift_g = second_pull(cotangent.astype(jnp.float32))
    outer_low = second_grad.astype(jnp.bfloat16)
    outer_bias_g = jnp.sum(outer_low.astype(jnp.float32), axis=0)
    outer_weight_g = contract_rows(activated, outer_low)
    act_grad = times_transposed(outer_low, outer)
    gelu_out, gelu_pull = jax.vjp(exact_gelu, inner_act)
    inner_low = gelu_pull(act_grad)[0].astype(jnp.bfloat16)
    inner_bias_g = jnp.sum(inner_low.astype(jnp.float32), axis=0)
    inner_weight_g = contract_rows(first_low, inner_low)
    first_total = second_grad + times_transposed(inner_low, inner)
    first_out, first_pull = jax.vjp(normalize, first_sum, vector_full[:, 3], vector_full[:, 4])
    first_grad, first_gain_g, first_shift_g = first_pull(first_total)
    attended_low = first_grad.astype(jnp.bfloat16)
    attn_bias_g = jnp.sum(attended_low.astype(jnp.float32), axis=0)
    attn_weight_g = contract_rows(context, attended_low)
    context_low = times_transposed(attended_low, attn).astype(jnp.bfloat16)
    split = split_heads(projected, keep.shape[0])
    queries = split[:, :, 0]
    keysets = split[:, :, 1]
    valuesets = split[:, :, 2]
    probs = attention_probs(queries, keysets, keep, scale)
    probs_low = probs.astype(jnp.bfloat16)
    context_heads = context_low.reshape(queries.shape)
    prob_grad = jnp.einsum(
        "sqhd,skhd->shqk", context_heads, valuesets, preferred_element_type=jnp.float32
    )
    value_grad = jnp.einsum(
        "shqk,sqhd->skhd", probs_low, context_heads, preferred_element_type=jnp.float32
    )
    score_low = (probs * (prob_grad - jnp.sum(probs * prob_grad, axis=-1, keepdims=True))).astype(
        jnp.bfloat16
    )
    query_grad = (
        jnp.einsum("shqk,skhd->sqhd", score_low, keysets, preferred_element_type=jnp.float32)
        * scale
    )
    key_grad = (
        jnp.einsum("shqk,sqhd->skhd", score_low, queries, preferred_element_type=jnp.float32)
        * scale
    )
    merged_low = jnp.stack((query_grad, key_grad, value_grad), axis=2).astype(jnp.bfloat16)
    merged_low = merged_low.reshape(rows.shape[0], 3 * width)
    merged_weight_g = contract_rows(rows, merged_low)
    merged_bias_g = jnp.sum(merged_low.astype(jnp.float32), axis=0)
    states_part = first_grad + times_transposed(merged_low, merged)
    vector_grads = jnp.stack(
        (
            merged_bias_g[:width],
            merged_bias_g[2 * width :],
            attn_bias_g,
            first_gain_g,
            first_shift_g,
            outer_bias_g,
            second_gain_g,
            second_shift_g,
        ),
        axis=1,
    )
    return (
        states_part,
        (
            merged_weight_g,
            attn_weight_g,
            inner_weight_g,
            outer_weight_g,
            vector_grads,
            inner_bias_g,
        ),
    )


def pack_vectors(vectors, widened):
    joined = jnp.concatenate(list(vectors) + [widened]).astype(jnp.float32)
    rows = joined.shape[0] // 128
    return jnp.pad(joined.reshape(rows, 128), ((0, 8 - rows), (0, 0)))


def shards(depth, *arrays):
    (states, pad_mask, query_proj, key_proj, value_proj, attn_proj, query_bias, value_bias, attn_bias, first_gain,
     first_shift, inner_proj, inner_bias, outer_proj, outer_bias, second_gain, second_shift, out_grad) = arrays
    width = states.shape[1]
    short = (query_bias, value_bias, attn_bias, first_gain, first_shift, outer_bias, second_gain, second_shift)
    if depth:
        return kernel_shards(depth, short, states, pad_mask, query_proj, key_proj, value_proj, attn_proj, inner_proj,
                             inner_bias, outer_proj, out_grad)
    merged_shard = jnp.concatenate((query_proj, key_proj, value_proj), axis=1)
    fetched = collect(merged_shard, attn_proj, inner_proj, outer_proj, jnp.stack(short, axis=1), inner_bias)
    encoded, kept = forward_pass(states, pad_mask, fetched)
    states_part, totals = backward_pass(states, pad_mask, out_grad, fetched, kept)
    merged_sum, attn_sum, inner_sum, outer_sum, vector_sum, widened_sum = reduce_grads(*totals)
    return ordered(encoded, states_part, merged_sum, attn_sum, inner_sum, outer_sum, vector_sum.T, widened_sum)


def ordered(encoded, states_part, merged_sum, attn_sum, inner_sum, outer_sum, vectors, widened_sum):
    width = attn_sum.shape[1]
    return (encoded, states_part, merged_sum[:, :width], merged_sum[:, width : 2 * width], merged_sum[:, 2 * width :],
            attn_sum, vectors[0], vectors[1], vectors[2], vectors[3], vectors[4], inner_sum, widened_sum, outer_sum,
            vectors[5], vectors[6], vectors[7])


def kernel_shards(depth, short, states, pad_mask, query_proj, key_proj, value_proj, attn_proj, inner_proj, inner_bias,
                  outer_proj, out_grad):
    width = states.shape[1]
    block = short[0].shape[0]
    long_block = inner_bias.shape[0]
    packed = pack_vectors(short, inner_bias)
    (merged, attn, inner, outer, encoded, projected, probs, context, first_sum, first_low, activated, slope, second_grad,
     outer_low, vectors, sums) = forward_all(
        depth, block, states, pad_mask, out_grad,
        (query_proj, key_proj, value_proj, attn_proj, inner_proj, outer_proj, packed))
    states_part, outer_sum, inner_sum, query_sum, key_sum, value_sum, attn_sum, table_sum = backward_all(
        depth, block, vectors, sums,
        (states, activated, slope, outer_low, second_grad, first_sum, first_low, context, projected, probs,
         merged.reshape(width, -1), attn.reshape(width, -1), inner, outer))
    joined = table_sum.reshape(-1)
    vector_sum = joined[: 8 * block].reshape(8, block)
    widened_sum = joined[8 * block : 8 * block + long_block]
    return (encoded, states_part, query_sum, key_sum, value_sum, attn_sum, vector_sum[0], vector_sum[1], vector_sum[2],
            vector_sum[3], vector_sum[4], inner_sum, widened_sum, outer_sum, vector_sum[5], vector_sum[6], vector_sum[7])


def solution(mesh):
    dps, others = mesh.shape["dp"], mesh.shape["fsdp"]
    matrix = P(("dp", "fsdp"), None)
    vector = P(("dp", "fsdp"))

    def whole(*arrays):
        rows = arrays[2].shape[0] // (dps * others)
        depth = others // 2 if rows % 16 == 0 and dps == 4 and others % 2 == 0 else 0
        return jax.shard_map(
            functools.partial(shards, depth),
            mesh=mesh,
            in_specs=(matrix,) * 6 + (vector,) * 5 + (matrix, vector, matrix) + (vector,) * 3 + (matrix,),
            out_specs=(matrix,) * 6 + (vector,) * 5 + (matrix, vector, matrix) + (vector,) * 3,
            check_vma=False,
        )(*arrays)

    return whole
```

profile of v0, /device:TPU:0, one launch (start us, length us, event | category | flops | bytes accessed | tf_op | source)
XLA Modules:
  0.0 317.7 jit_solution(14529019173837944085)
XLA Ops:
  0.7 6.1 %concatenate.3 = bf16[384]{0:T(512)(128)(2,1)S(1)} concatenate(bf16[32]{0:T(256)(128)(2,1)} %param.24, bf16[32]{0:T(256)(128)(2,1)} %param.25, bf16[32]{0:T(256)(128)(2,1)} %param.26, bf16[32]{0:T(256)(128)(2,1)} %param.27, bf16[32]{0:T(256)(128)(2,1)} %param.28, bf16[32]{0:T(256)(128)(2,1)} %param.32, bf16[32]{0:T(256)(128)(2,1)} %param.33, bf16[32]{0:T(256)(128)(2,1)} %param.34, ...), dimensions={0} | concatenate | bytes 1536 | tf_op jit(solution)/shard_map/concatenate | solution.py:1193
  6.8 0.6 pad_convert_fusion.refs_9_
  7.4 143.7 %forward.1 = (bf16[4,4,2,32,3072]{4,3,2,1,0:T(8,128)(2,1)}, bf16[4,4,2,32,1024]{4,3,2,1,0:T(8,128)(2,1)}, bf16[4,4,2,32,4096]{4,3,2,1,0:T(8,128)(2,1)}, bf16[4,4...) custom-call(bf16[512,1024]{1,0:T(8,128)(2,1)} %refs_2_.3, ...), custom_call_target="tpu_custom_call" | custom-call | tf_op jit(solution)/shard_map/forward/pallas_call | solution.py:499
  151.1 0.0 copy-start.1
  151.1 157.4 %backward.1 = (f32[512,1024]{1,0:T(8,128)}, f32[128,1024]{1,0:T(8,128)}, f32[32,4096]{1,0:T(8,128)}, f32[32,1024]{1,0:T(8,128)}, f32[32,1024]{1,0:T(8,128)}, /*i...) custom-call(f32[8,1024]{1,0:T(8,128)} %get-tuple-element.42.refs_0_, f32[8,1024]{1,0:T(8,128)} %get-tuple-element.43.refs_1_, ...), custom_call_target="tpu_custom_call" | custom-call | tf_op jit(solution)/shard_map/backward/pallas_call | solution.py:1010
  308.5 0.0 copy-start
  308.5 1.3 slice_bitcast_fusion.3
  309.9 0.7 slice.34
  310.6 0.1 reshape.53
  310.6 0.5 slice_bitcast_fusion
  311.2 0.0 copy-done.1
  311.2 0.0 copy-start.7
  311.2 0.0 copy-start.6
  311.2 0.0 copy-start.5
  311.2 0.0 copy-start.4
  311.2 0.0 copy-start.3
  311.2 1.0 copy.43
  312.2 0.0 copy-done
  312.2 0.0 copy-start.2
  312.2 1.3 copy.44
  313.5 0.0 copy-done.7
  313.5 0.7 copy.45
  314.2 0.0 copy-done.6
  314.2 0.7 copy.46
  314.8 0.0 copy-done.5
  314.8 0.7 copy.47
  315.5 0.0 copy-done.4
  315.5 0.7 copy.48
  316.2 0.0 copy-done.3
  316.2 0.8 copy.49
  317.0 0.0 copy-done.2
  317.0 0.8 copy.50
Async XLA Ops:
  151.1 160.1 %copy-start.1 = (bf16[512,1024]{1,0:T(8,128)(2,1)S(1)}, bf16[512,1024]{1,0:T(8,128)(2,1)}, u32[]{:S(2)}) copy-start(bf16[512,1024]{1,0:T(8,128)(2,1)} %get-tuple-element.90) | copy-start | bytes 3145732
  308.5 3.7 %copy-start = (f32[512,1024]{1,0:T(8,128)S(1)}, f32[512,1024]{1,0:T(8,128)}, u32[]{:S(2)}) copy-start(f32[512,1024]{1,0:T(8,128)} %get-tuple-element.91) | copy-start | bytes 6291460
  311.2 2.3 copy-start.7
  311.2 3.0 copy-start.6
  311.2 3.6 %copy-start.5 = (f32[32,1024]{1,0:T(8,128)S(1)}, f32[32,1024]{1,0:T(8,128)}, u32[]{:S(2)}) copy-start(f32[32,1024]{1,0:T(8,128)} %get-tuple-element.94) | copy-start | bytes 393220
  311.2 4.3 %copy-start.4 = (f32[32,1024]{1,0:T(8,128)S(1)}, f32[32,1024]{1,0:T(8,128)}, u32[]{:S(2)}) copy-start(f32[32,1024]{1,0:T(8,128)} %get-tuple-element.95) | copy-start | bytes 393220
  311.2 4.9 %copy-start.3 = (f32[32,4096]{1,0:T(8,128)S(1)}, f32[32,4096]{1,0:T(8,128)}, u32[]{:S(2)}) copy-start(f32[32,4096]{1,0:T(8,128)} %get-tuple-element.101) | copy-start | bytes 1572868
  312.2 4.8 %copy-start.2 = (f32[128,1024]{1,0:T(8,128)S(1)}, f32[128,1024]{1,0:T(8,128)}, u32[]{:S(2)}) copy-start(f32[128,1024]{1,0:T(8,128)} %get-tuple-element.103) | copy-start | bytes 1572868
where the time goes:
time: 318 us
  Pallas kernels  301 us (95%)
  local copies, waits for them, and re-layouts  15.3 us (5%)
    pallas_call x1, Pallas kernels, backward_all(): pl.pallas_call(functools.partial(backward_kernel, depth, block), out_shap...  157 us
    pallas_call x1, Pallas kernels, forward_all(): pl.pallas_call(functools.partial(forward_kernel, depth, block), out_shape...  144 us
    unnamed x24, local copies, waits for them, and re-layouts  6.53 us

commit v1 on v0

--- a/solution.py
+++ b/solution.py
@@ -103,9 +103,20 @@
         p = self.place
         pl.when(p.z < p.depth - 1)(lambda: self.copy_up(p.z, True).start())
         pl.when(p.z > 0)(lambda: self.copy_down(p.z, True).start())
-        self.copy_near(p.z, True).start()
-        self.copy_far(0, p.z, True).start()
         self.copy_own().start()
+
+    def send(self, step):
+        p = self.place
+
+        def act(z, first=False):
+            self.copy_near(z, first).start()
+            self.copy_far(0, z, first).start()
+
+        if step == 0:
+            act(p.z, True)
+        else:
+            pl.when(p.z >= step)(lambda: act(p.z - step))
+            pl.when(p.z + step < p.depth)(lambda: act(p.z + step))
 
     def hop(self, step):
         p = self.place
@@ -115,16 +126,12 @@
             z = p.z - step
             self.copy_up(z).wait_recv()
             pl.when(p.z < p.depth - 1)(lambda: self.copy_up(z).start())
-            self.copy_near(z).start()
-            self.copy_far(0, z).start()
 
         @pl.when(p.z + step < p.depth)
         def _():
             z = p.z + step
             self.copy_down(z).wait_recv()
             pl.when(p.z > 0)(lambda: self.copy_down(z).start())
-            self.copy_near(z).start()
-            self.copy_far(0, z).start()
 
     def last_hop(self):
         self.hop(self.place.depth - 1)
@@ -194,35 +201,41 @@
     return pl.ds(pl.multiple_of(index * size, size), size)
 
 
-def unpack_table(table, block, vectors):
-    places = table.shape[0] * table.shape[1] * table.shape[2]
+def unpack_table(table, block, vectors, long_bias):
+    dps, depth, cores = table.shape[:3]
+    places = dps * depth * cores
     width = vectors.shape[1]
-    per_row = 128 // block
     lane = lax.broadcasted_iota(jnp.int32, (128, width), 1)
     source = lax.broadcasted_iota(jnp.int32, (128, width), 0)
+    pick = jnp.where(source == lax.rem(lane, block), 1.0, 0.0).astype(jnp.bfloat16)
     owner = lax.broadcasted_iota(jnp.int32, (places, width), 1) // block
     mine = owner == lax.broadcasted_iota(jnp.int32, (places, width), 0)
+    blocks = [table[:, :, :, vector, :].reshape(places, 128) for vector in range(8)]
+    spread = matmul(jnp.concatenate(blocks, axis=0).astype(jnp.bfloat16), pick)
     for vector in range(8):
-        row = table[:, :, :, vector // per_row, :].reshape(places, 128).astype(jnp.bfloat16)
-        pick = jnp.where(source == lax.rem(lane, block) + block * (vector % per_row), 1.0, 0.0).astype(jnp.bfloat16)
-        spread = jnp.where(mine, matmul(row, pick), 0.0)
-        vectors[vector : vector + 1, :] = jnp.sum(spread, axis=0, keepdims=True)
+        own = jnp.where(mine, spread[vector * places : (vector + 1) * places], 0.0)
+        vectors[vector : vector + 1, :] = jnp.sum(own, axis=0, keepdims=True)
+    for index in range(places):
+        dp, z, core = index // (depth * cores), index // cores % depth, index % cores
+        long_bias[:, index * 128 : (index + 1) * 128] = table[dp, z, core, 8:9, :]
+
+
+CHUNK = 256
 
 
 def project(rows, weights, vectors, projected):
-    width = rows.shape[1]
+    chunks = rows.shape[1] // CHUNK
     for part, bias in ((0, 0), (1, None), (2, 1)):
 
         def one(index, _):
-            at = span(index, 256)
-            weight = flat(weights[:, :, :, :, part * width : (part + 1) * width])
-            total = matmul(rows[at, :], weight)
+            at = span(part * chunks + index, CHUNK)
+            total = matmul(rows[...], flat(weights[:, :, :, :, at]))
             if bias is not None:
-                total = total + vectors[bias : bias + 1, :]
-            projected[at, part * width : (part + 1) * width] = total.astype(jnp.bfloat16)
+                total = total + vectors[bias : bias + 1, span(index, CHUNK)]
+            projected[:, at] = total.astype(jnp.bfloat16)
             return 0
 
-        lax.fori_loop(0, rows.shape[0] // 256, one, 0)
+        lax.fori_loop(0, chunks, one, 0)
 
 
 def head_lanes(heads, rows, size):
@@ -245,10 +258,10 @@
 QUAD = 4
 
 
-def attend(projected, keep, probs, context):
+def attend(projected, keep, probs, context, first, last):
     width = context.shape[1]
     size = width // HEADS
-    segments, length = keep.shape
+    length = keep.shape[1]
     scale = size ** (-0.5)
     lanes = head_lanes(QUAD, length, size)
     quads = HEADS // QUAD
@@ -269,7 +282,7 @@
         context[at, span(quad, QUAD * size)] = merge_heads(matmul(low, valuesets), lanes).astype(jnp.bfloat16)
         return 0
 
-    lax.fori_loop(0, segments * quads, one, 0)
+    lax.fori_loop(first, last, one, 0)
 
 
 def center_scale(hidden):
@@ -280,54 +293,48 @@
 
 
 def first_block(rows, context, weights, vectors, first_sum, first_norm, first_low):
+    def product(index, _):
+        at = span(index, CHUNK)
+        attended = matmul(context[...], flat(weights[:, :, :, :, at])) + vectors[2:3, at]
+        first_sum[:, at] = rows[:, at].astype(jnp.float32) + attended
+        return 0
+
+    lax.fori_loop(0, rows.shape[1] // CHUNK, product, 0)
 
     def one(index, _):
-        at = span(index, 128)
-        weight = flat(weights[...])
-        total = rows[at, :].astype(jnp.float32) + (matmul(context[at, :], weight) + vectors[2:3, :])
-        first_sum[at, :] = total
-        normed, _ = center_scale(total)
+        at = span(index, 64)
+        normed, _ = center_scale(first_sum[at, :])
         result = normed * vectors[3:4, :] + vectors[4:5, :]
         first_norm[at, :] = result
         first_low[at, :] = result.astype(jnp.bfloat16)
         return 0
 
-    lax.fori_loop(0, rows.shape[0] // 128, one, 0)
-
-
-def inner_block(first_low, weights, table, row_at, activated, slope):
-    count = first_low.shape[0]
-    biases = table.shape[0] * table.shape[1] * table.shape[2]
-    chunks = weights.shape[4] // 512
-    per_chunk = biases // chunks
-    rows_of = table[:, :, :, row_at, :].reshape(biases, 128)
-    for chunk in range(chunks):
-        columns = slice(chunk * 512, (chunk + 1) * 512)
-        first = chunk * per_chunk
-        bias = jnp.concatenate([rows_of[first + part : first + part + 1] for part in range(per_chunk)], axis=1)
-
-        def one(index, _):
-            at = span(index, 128)
-            value = matmul(first_low[at, :], flat(weights[:, :, :, :, columns])) + bias
-            share = 0.5 * (1.0 + lax.erf(value * (0.5**0.5)))
-            bell = jnp.exp(-0.5 * value * value) * ((0.5 / jnp.pi) ** 0.5)
-            activated[at, columns] = (value * share).astype(jnp.bfloat16)
-            slope[at, columns] = (share + value * bell).astype(jnp.bfloat16)
-            return 0
-
-        lax.fori_loop(0, count // 128, one, 0)
+    lax.fori_loop(0, rows.shape[0] // 64, one, 0)
+
+
+def inner_block(first_low, weights, long_bias, activated, slope, first, last):
+    def one(index, _):
+        at = span(index, CHUNK)
+        value = matmul(first_low[...], flat(weights[:, :, :, :, at])) + long_bias[:, at]
+        share = 0.5 * (1.0 + lax.erf(value * (0.5**0.5)))
+        bell = jnp.exp(-0.5 * value * value) * ((0.5 / jnp.pi) ** 0.5)
+        activated[:, at] = (value * share).astype(jnp.bfloat16)
+        slope[:, at] = (share + value * bell).astype(jnp.bfloat16)
+        return 0
+
+    lax.fori_loop(first, last, one, 0)
 
 
 def outer_part(activated, weights, row, total, fresh):
     size = weights.shape[1] * weights.shape[2] * weights.shape[3]
 
     def one(index, _):
-        at = span(index, 256)
-        value = matmul(activated[at, span(row, size)], flat(weights[row]))
-        total[at, :] = value if fresh else total[at, :] + value
+        at = span(index, CHUNK)
+        value = matmul(activated[:, span(row, size)], flat(weights[row, :, :, :, at]))
+        total[:, at] = value if fresh else total[:, at] + value
         return 0
 
-    lax.fori_loop(0, activated.shape[0] // 256, one, 0)
+    lax.fori_loop(0, total.shape[1] // CHUNK, one, 0)
 
 
 def norm_back(grad, normed, rate, gain):
@@ -341,7 +348,7 @@
     sums[...] = jnp.zeros_like(sums)
 
     def one(index, _):
-        at = span(index, 128)
+        at = span(index, 64)
         normed, rate = center_scale(first_norm[at, :] + (total[at, :] + vectors[5:6, :]))
         gain = vectors[6:7, :]
         encoded[at, :] = (normed * gain + vectors[7:8, :]).astype(jnp.bfloat16)
@@ -355,7 +362,7 @@
         sums[7:8, :] += jnp.sum(grad, axis=0, keepdims=True)
         return 0
 
-    lax.fori_loop(0, first_norm.shape[0] // 128, one, 0)
+    lax.fori_loop(0, first_norm.shape[0] // 64, one, 0)
 
 
 def forward_kernel(depth, block, *refs):
@@ -364,8 +371,8 @@
     (encoded_out, projected_out, probs_out, context_out, first_sum_out, first_low_out, activated_out, slope_out,
      second_grad_out, outer_low_out, vectors, sums) = refs[14:26]
     (merged_own, table, merged, attn, inner, outer, projected, probs, context, first_sum, first_norm, first_low, activated,
-     slope, total, encoded, second_grad, outer_low, save_sem) = refs[26:45]
-    sems = refs[45:]
+     slope, total, encoded, second_grad, outer_low, long_bias, save_sem) = refs[26:46]
+    sems = refs[46:]
     place = Place(depth)
     width = rows.shape[1]
     for part, own in enumerate((query_own, key_own, value_own)):
@@ -391,50 +398,68 @@
         else:
             net.hop(step)
 
+    def each(nets_of, *names, step):
+        for name in names:
+            for net in nets_of:
+                hop(net, step) if name == "hop" else getattr(net, name)(step)
+
     for net in front:
         net.start()
-    for step in range(1, depth):
-        for net in front:
-            hop(net, step)
-        if step == 1:
-            net_inner.start()
-        for net in front:
-            net.spread(step - 1)
-    for net in front:
-        net.spread(depth - 1)
-    hop(net_inner, 1)
+    each(front, "send", step=0)
+    each(front, "hop", "send", step=1)
+    net_inner.start()
+    each(front, "spread", step=0)
+    for step in range(2, depth):
+        each(front, "hop", "send", step=step)
+        each(front, "spread", step=step - 1)
+    net_inner.send(0)
+    net_outer.start()
+    net_inner.hop(1)
+    net_inner.send(1)
+    each(front, "spread", step=depth - 1)
     net_inner.spread(0)
-    net_outer.start()
+    net_outer.hop(1)
+    for step in range(2, depth - 1):
+        net_inner.hop(step)
+        net_inner.send(step)
+        net_inner.spread(step - 1)
     for net in front:
         net.arrive_far(0)
         net.arrive_far(1)
         net.arrive_core(0, 1, 2, 3)
     save(merged, merged_out)
     save(attn, attn_out)
-    unpack_table(table, block, vectors)
+    unpack_table(table, block, vectors, long_bias)
     project(rows, merged, vectors, projected)
     save(projected, projected_out)
-    for step in range(2, depth):
-        hop(net_inner, step)
-        net_inner.spread(step - 1)
+    for step in range(2, depth - 1):
+        net_outer.hop(step)
+    net_inner.last_hop()
+    net_inner.send(depth - 1)
+    net_inner.spread(depth - 2)
+    count = probs.shape[0]
+    attend(projected, keep, probs, context, 0, count // 2)
+    net_outer.last_hop()
     net_inner.spread(depth - 1)
-    attend(projected, keep, probs, context)
+    attend(projected, keep, probs, context, count // 2, count)
     save(probs, probs_out)
     save(context, context_out)
-    hop(net_outer, 1)
-    net_outer.spread(0)
     first_block(rows, context, attn, vectors, first_sum, first_norm, first_low)
     save(first_sum, first_sum_out)
     save(first_low, first_low_out)
-    for step in range(2, depth):
-        hop(net_outer, step)
-        net_outer.spread(step - 1)
-    net_outer.spread(depth - 1)
     net_inner.arrive_far(0)
+    for step in range(depth):
+        net_outer.send(step)
     net_inner.arrive_far(1)
     net_inner.arrive_core(0, 1, 2, 3)
     save(inner, inner_out)
-    inner_block(first_low, inner, table, 8 * block // 128, activated, slope)
+    chunks = inner.shape[4] // CHUNK
+    inner_block(first_low, inner, long_bias, activated, slope, 0, chunks // 2)
+    for step in range(depth // 2):
+        net_outer.spread(step)
+    inner_block(first_low, inner, long_bias, activated, slope, chunks // 2, chunks)
+    for step in range(depth // 2, depth):
+        net_outer.spread(step)
     save(activated, activated_out)
     save(slope, slope_out)
     net_outer.arrive_core(0)
@@ -493,6 +518,7 @@
     scratch += [held[name] for name in ("first_low", "activated", "slope")]
     scratch += [pltpu.VMEM((tokens, width), high)]
     scratch += [held[name] for name in ("encoded", "second_grad", "outer_low")]
+    scratch += [pltpu.VMEM((1, hidden), high)]
     scratch += [pltpu.SemaphoreType.DMA((len(full_shapes) + len(kept),))]
     here = pl.BlockSpec(memory_space=pltpu.VMEM)
     away = pl.BlockSpec(memory_space=pl.ANY)
@@ -593,10 +619,11 @@
         self.add(self.got_row(at), self.slots.core.at[at])
         if self.before:
             pl.semaphore_signal(self.core_free.at[at, self.sub], inc=1, device_id=(p.dp, p.sibling), device_id_type=MESH)
-        if at < 2:
-            if self.late_after:
-                pl.semaphore_wait(self.far_free.at[1 - at, self.sub], 1)
-            self.copy_far(1 - at).start()
+
+    def start_far(self, half):
+        if self.late_after:
+            pl.semaphore_wait(self.far_free.at[half, self.sub], 1)
+        self.copy_far(half).start()
 
     def add_far(self, half):
         p = self.place
@@ -671,32 +698,36 @@
     grads[row, :, :, part * lines : (part + 1) * lines, :] = value.astype(jnp.bfloat16).reshape(depth, cores, lines, width)
 
 
-def hidden_back(low, weights, slopes, bias_sum):
-    width = low.shape[1]
-    for part in range(SUBS):
-        bias_sum[:, part * width : (part + 1) * width] = jnp.zeros((1, width), jnp.float32)
-
-        def one(index, _):
-            at = span(index, 128)
-            value = matmul_nt(low[at, :], flat(weights[part])) * slopes[SUBS + part, at, :].astype(jnp.float32)
-            rounded = value.astype(jnp.bfloat16)
-            slopes[SUBS + part, at, :] = rounded
-            bias_sum[:, part * width : (part + 1) * width] += jnp.sum(rounded.astype(jnp.float32), axis=0, keepdims=True)
-            return 0
-
-        lax.fori_loop(0, low.shape[0] // 128, one, 0)
-
-
-def first_total_part(grad, inner_low, weights, part):
+def hidden_back(low, weights, slopes, bias_sum, part):
+    depth, cores, count, width = weights.shape[1:]
+    size = cores * count
+
+    def one(index, _):
+        at = span(index, size)
+        value = matmul_nt(low[...], flat(weights[part, index])) * slopes[SUBS + part, :, at].astype(jnp.float32)
+        rounded = value.astype(jnp.bfloat16)
+        slopes[SUBS + part, :, at] = rounded
+        total = jnp.sum(rounded.astype(jnp.float32), axis=0, keepdims=True)
+        bias_sum[:, pl.ds(pl.multiple_of(part * width + index * size, size), size)] = total
+        return 0
+
+    lax.fori_loop(0, depth, one, 0)
+
+
+def first_total_rows(grad, inner_low, weights):
     lines = weights.shape[3] // SUBS
+    size = grad.shape[1] // weights.shape[0]
 
     def one(index, _):
-        at = span(index, 128)
-        weight = flat(weights[:, :, :, part * lines : (part + 1) * lines, :])
-        grad[at, :] += matmul_nt(inner_low[SUBS + part, at, :], weight)
+        at = span(index, size)
+        total = grad[:, at]
+        for part in range(SUBS):
+            weight = flat(weights[index, :, :, part * lines : (part + 1) * lines, :])
+            total = total + matmul_nt(inner_low[SUBS + part], weight)
+        grad[:, at] = total
         return 0
 
-    lax.fori_loop(0, grad.shape[0] // 128, one, 0)
+    lax.fori_loop(0, weights.shape[0], one, 0)
 
 
 def first_back(first_sum, grad, low, vectors, sums):
@@ -720,12 +751,14 @@
 
 
 def context_back(low, weights, context):
+    halves = weights.shape[1] // CHUNK
+
     def one(index, _):
-        at = span(index, 128)
-        context[at, :] = matmul_nt(low[at, :], flat(weights[0:2])).astype(jnp.bfloat16)
+        weight = weights[index // halves, span(lax.rem(index, halves), CHUNK), :]
+        context[:, span(index, CHUNK)] = matmul_nt(low[...], weight).astype(jnp.bfloat16)
         return 0
 
-    lax.fori_loop(0, low.shape[0] // 128, one, 0)
+    lax.fori_loop(0, context.shape[1] // CHUNK, one, 0)
 
 
 def attend_back(projected, probs, context_low, sums, first, last):
@@ -762,44 +795,39 @@
 
 def states_back(grad, projected, weights):
     width = grad.shape[1]
+    halves = weights.shape[1] // CHUNK
 
     def one(index, _):
-        at = span(index, 128)
-        total = grad[at, :]
+        at = span(index, CHUNK)
+        total = grad[:, at]
         for part in range(3):
-            weight = flat(weights[2 + 2 * part : 4 + 2 * part])
-            total = total + matmul_nt(projected[at, part * width : (part + 1) * width], weight)
-        grad[at, :] = total
+            weight = weights[2 + 2 * part + index // halves, span(lax.rem(index, halves), CHUNK), :]
+            total = total + matmul_nt(projected[:, part * width : (part + 1) * width], weight)
+        grad[:, at] = total
         return 0
 
-    lax.fori_loop(0, grad.shape[0] // 128, one, 0)
+    lax.fori_loop(0, width // CHUNK, one, 0)
 
 
 def pack_sums(sums, bias_sum, block, table):
     dps, depth, cores = table.shape[:3]
     places = dps * depth * cores
     width = sums.shape[1]
-    per_row = 128 // block
     lane = lax.broadcasted_iota(jnp.int32, (width, 128), 1)
     source = lax.broadcasted_iota(jnp.int32, (width, 128), 0)
+    pick = jnp.where(lane == lax.rem(source, block), 1.0, 0.0).astype(jnp.bfloat16)
     owner = lax.broadcasted_iota(jnp.int32, (places, width), 1) // block
     mine = owner == lax.broadcasted_iota(jnp.int32, (places, width), 0)
+    values = jnp.concatenate([jnp.where(mine, sums[vector : vector + 1, :], 0.0) for vector in range(8)], axis=0)
+    upper = values.astype(jnp.bfloat16)
+    lower = (values - upper.astype(jnp.float32)).astype(jnp.bfloat16)
+    total = matmul(upper, pick) + matmul(lower, pick)
     table[...] = jnp.zeros_like(table)
-    for row in range(8 // per_row):
-        total = jnp.zeros((places, 128), jnp.float32)
-        for part in range(per_row):
-            vector = row * per_row + part
-            pick = jnp.where(lane == lax.rem(source, block) + block * part, 1.0, 0.0).astype(jnp.bfloat16)
-            value = jnp.where(mine, sums[vector : vector + 1, :], 0.0)
-            upper = value.astype(jnp.bfloat16)
-            lower = (value - upper.astype(jnp.float32)).astype(jnp.bfloat16)
-            both = matmul(jnp.concatenate((upper, lower), axis=0), pick)
-            total = total + (both[:places] + both[places:])
-        table[:, :, :, row, :] = total.reshape(dps, depth, cores, 128)
-    row = 8 * block // 128
+    for vector in range(8):
+        table[:, :, :, vector, :] = total[vector * places : (vector + 1) * places].reshape(dps, depth, cores, 128)
     for index in range(places):
         dp, z, core = index // (depth * cores), index // cores % depth, index % cores
-        table[dp, z, core, row : row + 1, :] = bias_sum[:, index * 128 : (index + 1) * 128]
+        table[dp, z, core, 8:9, :] = bias_sum[:, index * 128 : (index + 1) * 128]
 
 
 def backward_kernel(depth, block, *refs):
@@ -861,33 +889,55 @@
     ]
     attn_net = others[3]
     mergeds = others[:3]
-    small = Scatter(place, table, table_slots, sems, credits, 3 * SUBS, 0, 0, 8)
+    small = Scatter(place, table, table_slots, sems, credits, 3 * SUBS, 0, 0, 16)
     row_order = (place.both, place.near, place.far, place.dp)
     sums[...] = known[...]
     sums[0:2, :] = jnp.zeros((2, width), jnp.float32)
     place.greet()
 
-    def pieces(nets, compute):
+    def pieces(nets, compute, early=()):
+        def added(at):
+            for net in nets:
+                net.add_core(at)
+            if at < 2:
+                for net in early:
+                    net.start_far(1 - at)
+
         for at in range(4):
             compute(row_order[at])
             for net in nets:
                 net.start_core(at)
             if at:
-                for net in nets:
-                    net.add_core(at - 1)
-        for net in nets:
-            net.add_core(3)
+                added(at - 1)
+        added(3)
+
+    order = outers + inners + [attn_net] + mergeds + [small]
+    outs = [outer_out.at[pl.ds(sub * lines, lines), :] for sub in range(SUBS)]
+    outs += [inner_out.at[:, pl.ds(sub * width, width)] for sub in range(SUBS)]
+    outs += [attn_out, query_out, key_out, value_out, table_out]
+    window = 3
+
+    def pump(number):
+        if number < len(order):
+            order[number].add_far(1)
+            order[number].add_far(0)
+        if number + window < len(order):
+            order[number + window].start_far(1)
+            order[number + window].start_far(0)
+        if 1 <= number <= len(order):
+            order[number - 1].add_near()
+        if 3 <= number:
+            order[number - 3].finish(outs[number - 3])
 
     low_load.wait()
     for copy in act_loads:
         copy.wait()
-    pieces(outers, lambda row: outer_gradient(wide, low, outer_grads, row))
-    half = tokens
-    attn_loads = [load(attn_in.at[part * half : (part + 1) * half], wide.at[part]) for part in range(2)]
+    pieces(outers, lambda row: outer_gradient(wide, low, outer_grads, row), outers[:window])
+    attn_loads = [load(attn_in.at[part * tokens : (part + 1) * tokens], wide.at[part]) for part in range(2)]
 
     def load_merged(part):
         return [
-            load(merged_in.at[at * half : (at + 1) * half, part * width : (part + 1) * width], wide.at[2 + 2 * part + at])
+            load(merged_in.at[at * tokens : (at + 1) * tokens, part * width : (part + 1) * width], wide.at[2 + 2 * part + at])
             for at in range(2)
         ]
 
@@ -895,39 +945,36 @@
     outer_load.wait()
     for copy in slope_loads:
         copy.wait()
-    hidden_back(low, first_buffer, wide, bias_sum)
+    for part in range(SUBS):
+        hidden_back(low, first_buffer, wide, bias_sum, part)
     first_low_load.wait()
 
     def inner_rows(row):
         for part in range(SUBS):
             input_gradient(first_low, wide[SUBS + part], inner_grads, row, part)
 
+    pump(0)
     pieces(inners, inner_rows)
-    for net in outers:
-        net.add_far(1)
+    pump(1)
     grad_load.wait()
     for copy in inner_loads:
         copy.wait()
-    for part in range(SUBS):
-        first_total_part(grad, wide, second_buffer, part)
+    first_total_rows(grad, wide, second_buffer)
     merged_loads += load_merged(1) + load_merged(2)
-    for net in outers:
-        net.add_far(0)
     first_sum_load.wait()
     first_back(first_sum, grad, low, vectors, sums)
+    pump(2)
     context_load.wait()
     pieces([attn_net], lambda row: input_gradient(context, low[...], other_grads, row, 3))
     for copy in attn_loads:
         copy.wait()
     context_back(low, wide, context)
-    for net in outers:
-        net.add_near()
     projected_load.wait()
     probs_load.wait()
+    pump(3)
     count = probs.shape[0]
     attend_back(projected, probs, context, sums, 0, count // 2)
-    for net in inners:
-        net.add_far(1)
+    pump(4)
     attend_back(projected, probs, context, sums, count // 2, count)
     rows_load.wait()
 
@@ -935,31 +982,19 @@
         for part in range(3):
             input_gradient(rows, projected[:, part * width : (part + 1) * width], other_grads, row, part)
 
-    for sub, net in enumerate(outers):
-        net.finish(outer_out.at[pl.ds(sub * lines, lines), :])
     pieces(mergeds, merged_rows)
-    for net in inners:
-        net.add_far(0)
+    pump(5)
     pack_sums(sums, bias_sum, block, table)
     pieces([small], lambda row: None)
+    pump(6)
     for copy in merged_loads:
         copy.wait()
     states_back(grad, projected, wide)
     save = pltpu.make_async_copy(grad, states_out, save_sem)
     save.start()
-    for net in inners:
-        net.add_near()
-    last = [attn_net] + mergeds + [small]
-    for net in last:
-        net.add_far(1)
-    for net in last:
-        net.add_far(0)
-        net.add_near()
-    for sub, net in enumerate(inners):
-        net.finish(inner_out.at[:, pl.ds(sub * width, width)])
-    for net, out in zip(last, (attn_out, query_out, key_out, value_out, table_out)):
-        net.finish(out)
-    for net in outers + inners + last:
+    for number in range(7, len(order) + 3):
+        pump(number)
+    for net in order:
         net.drain()
     save.wait()
 
@@ -993,18 +1028,18 @@
         pltpu.VMEM((tokens, width), low),
         pltpu.VMEM((8, width), high),
         pltpu.VMEM((1, hidden), high),
-        pltpu.VMEM((4, depth, 2, 8, 128), high),
-        pltpu.VMEM((4, depth, 8, 128), high),
-        pltpu.VMEM((1, 2, depth, 8, 128), high),
-        pltpu.VMEM((1, depth, 8, 128), high),
-        pltpu.VMEM((1, depth - 1, 8, 128), high),
+        pltpu.VMEM((4, depth, 2, 16, 128), high),
+        pltpu.VMEM((4, depth, 16, 128), high),
+        pltpu.VMEM((1, 2, depth, 16, 128), high),
+        pltpu.VMEM((1, depth, 16, 128), high),
+        pltpu.VMEM((1, depth - 1, 16, 128), high),
         dma((40,)),
         dma,
         dma((nets, 4)), dma((nets, 4)), dma((nets, 2)), dma((nets, 2)), dma((nets,)), dma((nets,)),
         dma((nets, depth - 1)), dma((nets, depth - 1)),
         regular((4, SUBS)), regular((2, SUBS)), regular((SUBS,)), regular((SUBS, depth - 1)),
     ]
-    shapes = [(tokens, width), (lines, width), (own_rows, hidden)] + [(own_rows, width)] * 4 + [(8, 128)]
+    shapes = [(tokens, width), (lines, width), (own_rows, hidden)] + [(own_rows, width)] * 4 + [(16, 128)]
     here = pl.BlockSpec(memory_space=pltpu.VMEM)
     away = pl.BlockSpec(memory_space=pl.ANY)
     return pl.pallas_call(
@@ -1189,10 +1224,13 @@
     )
 
 
-def pack_vectors(vectors, widened):
-    joined = jnp.concatenate(list(vectors) + [widened]).astype(jnp.float32)
-    rows = joined.shape[0] // 128
-    return jnp.pad(joined.reshape(rows, 128), ((0, 8 - rows), (0, 0)))
+def pack_vectors(vectors):
+    row = lax.broadcasted_iota(jnp.int32, (16, 128), 0)
+    table = jnp.zeros((16, 128), jnp.float32)
+    for index, vector in enumerate(vectors):
+        padded = jnp.pad(vector.astype(jnp.float32), (0, 128 - vector.shape[0]))
+        table = jnp.where(row == index, padded[None, :], table)
+    return table
 
 
 def shards(depth, *arrays):
@@ -1222,8 +1260,7 @@
                   outer_proj, out_grad):
     width = states.shape[1]
     block = short[0].shape[0]
-    long_block = inner_bias.shape[0]
-    packed = pack_vectors(short, inner_bias)
+    packed = pack_vectors(short + (inner_bias,))
     (merged, attn, inner, outer, encoded, projected, probs, context, first_sum, first_low, activated, slope, second_grad,
      outer_low, vectors, sums) = forward_all(
         depth, block, states, pad_mask, out_grad,
@@ -1232,11 +1269,10 @@
         depth, block, vectors, sums,
         (states, activated, slope, outer_low, second_grad, first_sum, first_low, context, projected, probs,
          merged.reshape(width, -1), attn.reshape(width, -1), inner, outer))
-    joined = table_sum.reshape(-1)
-    vector_sum = joined[: 8 * block].reshape(8, block)
-    widened_sum = joined[8 * block : 8 * block + long_block]
-    return (encoded, states_part, query_sum, key_sum, value_sum, attn_sum, vector_sum[0], vector_sum[1], vector_sum[2],
-            vector_sum[3], vector_sum[4], inner_sum, widened_sum, outer_sum, vector_sum[5], vector_sum[6], vector_sum[7])
+    short_sums = [table_sum[index, :block] for index in range(8)]
+    widened_sum = table_sum[8, : inner_bias.shape[0]]
+    return (encoded, states_part, query_sum, key_sum, value_sum, attn_sum, *short_sums[:5], inner_sum, widened_sum,
+            outer_sum, *short_sums[5:])
 
 
 def solution(mesh):
@@ -1246,7 +1282,8 @@
 
     def whole(*arrays):
         rows = arrays[2].shape[0] // (dps * others)
-        depth = others // 2 if rows % 16 == 0 and dps == 4 and others % 2 == 0 else 0
+        tiles = rows % 16 == 0 and arrays[12].shape[0] == 128 * dps * others
+        depth = others // 2 if tiles and dps == 4 and others % 2 == 0 else 0
         return jax.shard_map(
             functools.partial(shards, depth),
             mesh=mesh,

time: 318 us -> 272 us (0.86)
  Pallas kernels: 301 us -> 257 us
  local copies, waits for them, and re-layouts: 15.3 us -> 9.38 us
  other arithmetic: 0.6 us -> 4.08 us
    pallas_call x1, Pallas kernels: 157 us -> 127 us  [backward_all(): pl.pallas_call(functools.partial(backward_kernel, depth, block), out_shap...]
    pallas_call x1, Pallas kernels: 144 us -> 130 us  [forward_all(): pl.pallas_call(functools.partial(forward_kernel, depth, block), out_shape...]
    concatenate x1 -> x0, local copies, waits for them, and re-layouts: 6.09 us -> none  [pack_vectors(): joined = jnp.concatenate(list(vectors) + [widened]).astype(jnp.float32)]
where the time goes in v1:
time: 272 us
  Pallas kernels  257 us (94%)
  local copies, waits for them, and re-layouts  9.38 us (3%)
  other arithmetic  4.08 us (2%)
    pallas_call x1, Pallas kernels, forward_all(): pl.pallas_call(functools.partial(forward_kernel, depth, block), out_shape...  130 us
    pallas_call x1, Pallas kernels, backward_all(): pl.pallas_call(functools.partial(backward_kernel, depth, block), out_shap...  127 us
    unnamed x24, local copies, waits for them, and re-layouts  6.53 us

profile of v1, /device:TPU:0, one launch (start us, length us, event | category | flops | bytes accessed | tf_op | source)
XLA Modules:
  0.0 271.6 jit_solution(965027892837004076)
XLA Ops:
  0.7 0.7 convert_element_type.20
  1.3 0.7 pad_convert_fusion
  2.0 0.7 pad_convert_fusion.2
  2.7 0.7 pad_convert_fusion.4
  3.3 0.7 pad_convert_fusion.6
  4.1 0.7 select_select_fusion.refs_9_
  4.7 130.3 %forward.1 = (bf16[4,4,2,32,3072]{4,3,2,1,0:T(8,128)(2,1)}, bf16[4,4,2,32,1024]{4,3,2,1,0:T(8,128)(2,1)}, bf16[4,4,2,32,4096]{4,3,2,1,0:T(8,128)(2,1)}, bf16[4,4...) custom-call(bf16[512,1024]{1,0:T(8,128)(2,1)} %refs_2_.3, ...), custom_call_target="tpu_custom_call" | custom-call | tf_op jit(solution)/shard_map/forward/pallas_call | solution.py:525
  135.1 0.0 copy-start.1
  135.1 127.0 %backward.1 = (f32[512,1024]{1,0:T(8,128)}, f32[128,1024]{1,0:T(8,128)}, f32[32,4096]{1,0:T(8,128)}, f32[32,1024]{1,0:T(8,128)}, f32[32,1024]{1,0:T(8,128)}, /*i...) custom-call(f32[8,1024]{1,0:T(8,128)} %get-tuple-element.42.refs_0_, f32[8,1024]{1,0:T(8,128)} %get-tuple-element.43.refs_1_, ...), custom_call_target="tpu_custom_call" | custom-call | tf_op jit(solution)/shard_map/backward/pallas_call | solution.py:1045
  262.1 0.0 copy-start
  262.2 1.3 slice_bitcast_fusion.3
  263.5 1.5 slice_bitcast_fusion
  265.0 0.0 copy-done.1
  265.0 0.0 copy-start.7
  265.0 0.0 copy-start.6
  265.0 0.0 copy-start.5
  265.0 0.0 copy-start.4
  265.0 1.0 copy.43
  266.0 0.0 copy-done
  266.0 1.3 copy.44
  267.3 0.0 copy-done.7
  267.3 0.7 copy.45
  268.0 0.0 copy-done.6
  268.0 0.7 copy.46
  268.7 0.0 copy-done.5
  268.7 0.7 copy.47
  269.3 0.0 copy-done.4
  269.3 0.7 copy.48
  270.0 0.0 copy-done.3
  270.0 0.8 copy.49
  270.8 0.0 copy-done.2
  270.8 0.8 copy.50
  (7 shorter events, 0.0 us)
Async XLA Ops:
  135.1 129.9 %copy-start.1 = (bf16[512,1024]{1,0:T(8,128)(2,1)S(1)}, bf16[512,1024]{1,0:T(8,128)(2,1)}, u32[]{:S(2)}) copy-start(bf16[512,1024]{1,0:T(8,128)(2,1)} %get-tuple-element.106) | copy-start | bytes 3145732
  262.1 3.9 %copy-start = (f32[512,1024]{1,0:T(8,128)S(1)}, f32[512,1024]{1,0:T(8,128)}, u32[]{:S(2)}) copy-start(f32[512,1024]{1,0:T(8,128)} %get-tuple-element.107) | copy-start | bytes 6291460
  265.0 2.3 copy-start.7
  265.0 3.0 %copy-start.6 = (f32[32,1024]{1,0:T(8,128)S(1)}, f32[32,1024]{1,0:T(8,128)}, u32[]{:S(2)}) copy-start(f32[32,1024]{1,0:T(8,128)} %get-tuple-element.109) | copy-start | bytes 393220
  265.0 3.6 %copy-start.5 = (f32[32,1024]{1,0:T(8,128)S(1)}, f32[32,1024]{1,0:T(8,128)}, u32[]{:S(2)}) copy-start(f32[32,1024]{1,0:T(8,128)} %get-tuple-element.110) | copy-start | bytes 393220
  265.0 4.3 %copy-start.4 = (f32[32,1024]{1,0:T(8,128)S(1)}, f32[32,1024]{1,0:T(8,128)}, u32[]{:S(2)}) copy-start(f32[32,1024]{1,0:T(8,128)} %get-tuple-element.111) | copy-start | bytes 393220
  266.0 4.0 %copy-start.3 = (f32[32,4096]{1,0:T(8,128)S(1)}, f32[32,4096]{1,0:T(8,128)}, u32[]{:S(2)}) copy-start(f32[32,4096]{1,0:T(8,128)} %get-tuple-element.117) | copy-start | bytes 1572868
  266.0 4.8 %copy-start.2 = (f32[128,1024]{1,0:T(8,128)S(1)}, f32[128,1024]{1,0:T(8,128)}, u32[]{:S(2)}) copy-start(f32[128,1024]{1,0:T(8,128)} %get-tuple-element.119) | copy-start | bytes 1572868

commit v2 on v1

--- a/solution.py
+++ b/solution.py
@@ -29,6 +29,9 @@
         self.both = lax.rem(flip_x + 2, 4)
         self.fsdp = fsdp
         self.sibling = fsdp + 1 - 2 * self.core
+        self.pair = self.z + 1 - 2 * lax.rem(self.z, 2)
+        self.jump = self.up(2)
+        self.cross = 3 - self.z
 
     def up(self, step):
         return lax.rem(self.z + step, self.depth)
@@ -55,36 +58,37 @@
 
 
 class Gather:
-    def __init__(self, place, full, own, sems, piece):
-        self.place, self.full, self.own, self.piece = place, full, own, piece
+    def __init__(self, place, full, own, sems, piece, lines=None):
+        self.lines = pl.ds(0, full.shape[3]) if lines is None else lines
+        self.place, self.full, self.own, self.piece = place, full, own.at[self.lines], piece
         self.su, self.ru, self.sd, self.rd, self.sb, self.rb, self.sa, self.ra, self.sc, self.rc, self.so = sems
 
     def copy_own(self):
         p = self.place
-        return pltpu.make_async_copy(self.own, self.full.at[p.dp, p.z, p.core], self.so.at[self.piece])
+        return pltpu.make_async_copy(self.own, self.full.at[p.dp, p.z, p.core, self.lines], self.so.at[self.piece])
 
     def copy_up(self, z, first=False):
         p = self.place
-        block = self.full.at[p.dp, z, p.core]
+        block = self.full.at[p.dp, z, p.core, self.lines]
         source = self.own if first else block
         return remote(source, block, self.su.at[self.piece, z], self.ru.at[self.piece, z], p.along(p.z + 1))
 
     def copy_down(self, z, first=False):
         p = self.place
-        block = self.full.at[p.dp, z, p.core]
+        block = self.full.at[p.dp, z, p.core, self.lines]
         source = self.own if first else block
         return remote(source, block, self.sd.at[self.piece, z], self.rd.at[self.piece, z], p.along(p.z - 1))
 
     def copy_near(self, z, first=False, arriving=False):
         p = self.place
-        block = self.full.at[p.near if arriving else p.dp, z, p.core]
+        block = self.full.at[p.near if arriving else p.dp, z, p.core, self.lines]
         source = self.own if first else block
         return remote(source, block, self.sb.at[self.piece, z], self.rb.at[self.piece, z], (p.near, p.fsdp))
 
     def copy_far(self, half, z, first=False, arriving=False):
         p = self.place
         row = (p.both if half else p.far) if arriving else (p.near if half else p.dp)
-        block = self.full.at[row, z, p.core]
+        block = self.full.at[row, z, p.core, self.lines]
         source = self.own if first else block
         at = half * p.depth + z
         return remote(source, block, self.sa.at[self.piece, at], self.ra.at[self.piece, at], (p.far, p.fsdp))
@@ -93,10 +97,10 @@
         p = self.place
         if arriving:
             row = (p.dp, p.far, p.near, p.both)[part]
-            block = self.full.at[row, :, 1 - p.core]
+            block = self.full.at[row, :, 1 - p.core, self.lines]
         else:
             row = (p.dp, p.near, p.far, p.both)[part]
-            block = self.full.at[row, :, p.core]
+            block = self.full.at[row, :, p.core, self.lines]
         return remote(block, block, self.sc.at[self.piece, part], self.rc.at[self.piece, part], (p.dp, p.sibling))
 
     def start(self):
@@ -171,6 +175,88 @@
             self.copy_near(z).wait_send()
             self.copy_far(0, z).wait_send()
             self.copy_far(1, z).wait_send()
+        for part in range(4):
+            self.copy_core(part).wait_send()
+
+
+class GatherLine:
+    def __init__(self, place, full, own, sems, piece, lines):
+        self.place, self.full, self.own, self.piece, self.lines = place, full, own.at[lines], piece, lines
+        self.sj, self.rj, self.sp, self.rp, self.sb, self.rb, self.sa, self.ra, self.sc, self.rc, self.so = sems
+
+    def block(self, row):
+        return self.full.at[row, self.place.z, self.place.core, self.lines]
+
+    def column(self, z, core):
+        return self.full.at[:, z, core, self.lines]
+
+    def copy_own(self):
+        return pltpu.make_async_copy(self.own, self.block(self.place.dp), self.so.at[self.piece])
+
+    def copy_near(self, arriving=False):
+        p = self.place
+        target = self.block(p.near if arriving else p.dp)
+        return remote(self.own, target, self.sb.at[self.piece, 0], self.rb.at[self.piece, 0], (p.near, p.fsdp))
+
+    def copy_far(self, half, arriving=False):
+        p = self.place
+        target = self.block((p.both if half else p.far) if arriving else (p.near if half else p.dp))
+        source = target if half else self.own
+        return remote(source, target, self.sa.at[self.piece, half], self.ra.at[self.piece, half], (p.far, p.fsdp))
+
+    def copy_jump(self, arriving=False):
+        p = self.place
+        column = self.column(p.jump if arriving else p.z, p.core)
+        return remote(column, column, self.sj.at[self.piece, 0], self.rj.at[self.piece, 0], p.along(p.jump))
+
+    def copy_pair(self, part, arriving=False):
+        p = self.place
+        z = (p.cross if part else p.pair) if arriving else (p.jump if part else p.z)
+        column = self.column(z, p.core)
+        return remote(column, column, self.sp.at[self.piece, part], self.rp.at[self.piece, part], p.along(p.pair))
+
+    def copy_core(self, part, arriving=False):
+        p = self.place
+        column = self.column((p.z, p.jump, p.pair, p.cross)[part], 1 - p.core if arriving else p.core)
+        return remote(column, column, self.sc.at[self.piece, part], self.rc.at[self.piece, part], (p.dp, p.sibling))
+
+    def start(self):
+        self.copy_near().start()
+        self.copy_far(0).start()
+        self.copy_own().start()
+
+    def spread(self):
+        self.copy_near(arriving=True).wait_recv()
+        self.copy_far(1).start()
+
+    def join(self):
+        self.copy_own().wait()
+        for half in range(2):
+            self.copy_far(half, arriving=True).wait_recv()
+        self.copy_jump().start()
+        self.copy_pair(0).start()
+        self.copy_core(0).start()
+
+    def relay(self):
+        self.copy_jump(arriving=True).wait_recv()
+        self.copy_pair(1).start()
+        self.copy_core(1).start()
+
+    def arrive(self):
+        for part in range(2):
+            self.copy_pair(part, arriving=True).wait_recv()
+            self.copy_core(2 + part).start()
+
+    def arrive_core(self):
+        for part in range(4):
+            self.copy_core(part, arriving=True).wait_recv()
+
+    def drain(self):
+        self.copy_near().wait_send()
+        self.copy_jump().wait_send()
+        for part in range(2):
+            self.copy_far(part).wait_send()
+            self.copy_pair(part).wait_send()
         for part in range(4):
             self.copy_core(part).wait_send()
 
@@ -366,13 +452,17 @@
 
 
 def forward_kernel(depth, block, *refs):
-    (rows, keep, cotangent, query_own, key_own, value_own, attn_own, inner_own, outer_own, table_own) = refs[:10]
-    merged_out, attn_out, inner_out, outer_out = refs[10:14]
+    (rows, keep, cotangent, query_own, key_own, value_own, attn_own, inner_own, outer_own) = refs[:9]
+    short_vectors = refs[9:18]
+    merged_out, attn_out, inner_out, outer_out = refs[18:22]
     (encoded_out, projected_out, probs_out, context_out, first_sum_out, first_low_out, activated_out, slope_out,
-     second_grad_out, outer_low_out, vectors, sums) = refs[14:26]
-    (merged_own, table, merged, attn, inner, outer, projected, probs, context, first_sum, first_norm, first_low, activated,
-     slope, total, encoded, second_grad, outer_low, long_bias, save_sem) = refs[26:46]
-    sems = refs[46:]
+     second_grad_out, outer_low_out, vectors, sums) = refs[22:34]
+    (table_own, merged_own, table, merged, attn, inner, outer, projected, probs, context, first_sum, first_norm, first_low,
+     activated, slope, total, encoded, second_grad, outer_low, long_bias, save_sem) = refs[34:55]
+    sems = refs[55:]
+    table_own[...] = jnp.zeros_like(table_own)
+    for index, vector in enumerate(short_vectors):
+        table_own[index, : vector.shape[0]] = vector[...].astype(jnp.float32)
     place = Place(depth)
     width = rows.shape[1]
     for part, own in enumerate((query_own, key_own, value_own)):
@@ -381,8 +471,10 @@
     net_merged = Gather(place, merged, merged_own, sems, 1)
     net_attn = Gather(place, attn, attn_own, sems, 2)
     net_inner = Gather(place, inner, inner_own, sems, 3)
-    net_outer = Gather(place, outer, outer_own, sems, 4)
-    nets = (net_table, net_merged, net_attn, net_inner, net_outer)
+    half = outer.shape[3] // 2
+    net_outer = Gather(place, outer, outer_own, sems, 4, pl.ds(0, half))
+    line = GatherLine(place, outer, outer_own, sems, 5, pl.ds(half, half))
+    nets = (net_table, net_merged, net_attn, net_inner, net_outer, line)
     front = nets[:3]
     place.greet()
     saves = []
@@ -406,7 +498,9 @@
     for net in front:
         net.start()
     each(front, "send", step=0)
+    line.start()
     each(front, "hop", "send", step=1)
+    line.spread()
     net_inner.start()
     each(front, "spread", step=0)
     for step in range(2, depth):
@@ -423,6 +517,7 @@
         net_inner.hop(step)
         net_inner.send(step)
         net_inner.spread(step - 1)
+    line.join()
     for net in front:
         net.arrive_far(0)
         net.arrive_far(1)
@@ -437,6 +532,7 @@
     net_inner.last_hop()
     net_inner.send(depth - 1)
     net_inner.spread(depth - 2)
+    line.relay()
     count = probs.shape[0]
     attend(projected, keep, probs, context, 0, count // 2)
     net_outer.last_hop()
@@ -453,15 +549,23 @@
     net_inner.arrive_far(1)
     net_inner.arrive_core(0, 1, 2, 3)
     save(inner, inner_out)
-    chunks = inner.shape[4] // CHUNK
-    inner_block(first_low, inner, long_bias, activated, slope, 0, chunks // 2)
-    for step in range(depth // 2):
+    quarter = inner.shape[4] // CHUNK // 4
+
+    def inner_quarter(index):
+        inner_block(first_low, inner, long_bias, activated, slope, index * quarter, (index + 1) * quarter)
+
+    inner_quarter(0)
+    net_outer.spread(0)
+    inner_quarter(1)
+    for step in range(1, depth - 1):
         net_outer.spread(step)
-    inner_block(first_low, inner, long_bias, activated, slope, chunks // 2, chunks)
-    for step in range(depth // 2, depth):
-        net_outer.spread(step)
+    inner_quarter(2)
+    net_outer.spread(depth - 1)
+    line.arrive()
+    inner_quarter(3)
     save(activated, activated_out)
     save(slope, slope_out)
+    line.arrive_core()
     net_outer.arrive_core(0)
     outer_part(activated, outer, place.dp, total, True)
     net_outer.arrive_far(0)
@@ -483,7 +587,7 @@
 
 
 def forward_all(depth, block, rows, keep, cotangent, owns):
-    query_own, _, _, attn_own, inner_own, outer_own, table_own = owns
+    query_own, _, _, attn_own, inner_own, outer_own = owns[:6]
     tokens, width = rows.shape
     hidden = inner_own.shape[1]
     segments, length = keep.shape
@@ -511,7 +615,8 @@
     held = {name: pltpu.VMEM(*one) for name, one in zip(
         ("encoded", "projected", "probs", "context", "first_sum", "first_low", "activated", "slope", "second_grad", "outer_low"),
         kept)}
-    scratch = [pltpu.VMEM((query_own.shape[0], 3 * width), low), pltpu.VMEM(fulls(table_own, 128), high)]
+    scratch = [pltpu.VMEM((16, 128), high), pltpu.VMEM((query_own.shape[0], 3 * width), low)]
+    scratch += [pltpu.VMEM((4, depth, 2, 16, 128), high)]
     scratch += [pltpu.VMEM(shape, low) for shape in full_shapes]
     scratch += [held[name] for name in ("projected", "probs", "context", "first_sum")]
     scratch += [pltpu.VMEM((tokens, width), high)]
@@ -525,9 +630,9 @@
     return pl.pallas_call(
         functools.partial(forward_kernel, depth, block),
         out_shape=shapes,
-        in_specs=[here] * 10,
+        in_specs=[here] * (3 + len(owns)),
         out_specs=[away] * (len(full_shapes) + len(kept)) + [here] * 2,
-        scratch_shapes=scratch + gather_sems(5, depth),
+        scratch_shapes=scratch + gather_sems(6, depth),
         compiler_params=pltpu.CompilerParams(
             collective_id=0, has_side_effects=True, vmem_limit_bytes=60 * 1024 * 1024
         ),
@@ -676,6 +781,120 @@
         self.copy_near().wait_send()
         for step in range(1, self.place.depth):
             self.copy_z(step).wait_send()
+
+
+class ScatterLine(Scatter):
+    def column(self, z):
+        return self.whole.at[:, z, self.place.core, self.lines()]
+
+    def copy_pair(self, part):
+        p = self.place
+        return remote(
+            self.column(p.cross if part else p.pair), self.slots.far.at[0, part, :, self.lines()],
+            self.sa.at[self.number, part], self.ra.at[self.number, part], p.along(p.pair),
+        )
+
+    def copy_jump(self):
+        p = self.place
+        return remote(
+            self.column(p.jump), self.slots.near.at[0, :, self.lines()], self.sb.at[self.number], self.rb.at[self.number],
+            p.along(p.jump),
+        )
+
+    def copy_axis(self, part):
+        p = self.place
+        row = (p.both, p.far, p.near)[part]
+        target = p.near if part == 2 else p.far
+        return remote(
+            self.whole.at[row, p.z, p.core, self.lines()], self.slots.along.at[0, part, self.lines()],
+            self.sz.at[self.number, part], self.rz.at[self.number, part], (target, p.fsdp),
+        )
+
+    def add_column(self, z, slot):
+        p = self.place
+        tiles = self.count // self.tile
+
+        def one(index, _):
+            row = index // tiles
+            at = pl.ds(pl.multiple_of(self.first + lax.rem(index, tiles) * self.tile, self.tile), self.tile)
+            self.whole[row, z, p.core, at, :] = self.whole[row, z, p.core, at, :] + slot[row, at, :]
+            return 0
+
+        lax.fori_loop(0, self.whole.shape[0] * tiles, one, 0)
+
+    def add_block(self, row, part):
+        p = self.place
+
+        def one(index, _):
+            at = pl.ds(pl.multiple_of(self.first + index * self.tile, self.tile), self.tile)
+            self.whole[row, p.z, p.core, at, :] = self.whole[row, p.z, p.core, at, :] + self.slots.along[0, part, at, :]
+            return 0
+
+        lax.fori_loop(0, self.count // self.tile, one, 0)
+
+    def tell(self, semaphore, device):
+        pl.semaphore_signal(semaphore, inc=1, device_id=device, device_id_type=MESH)
+
+    def add_core(self, at):
+        p = self.place
+        self.copy_core(at).wait_recv()
+        self.add(self.got_row(at), self.slots.core.at[at])
+        for sub in range(SUBS // 2, SUBS):
+            self.tell(self.core_free.at[at, sub], (p.dp, p.sibling))
+
+    def start_pair(self):
+        self.copy_pair(1).start()
+        self.copy_pair(0).start()
+
+    def add_pair(self, part):
+        p = self.place
+        self.copy_pair(part).wait_recv()
+        self.add_column(p.jump if part else p.z, self.slots.far.at[0, part])
+        if part:
+            self.copy_jump().start()
+        for sub in range(SUBS // 2, SUBS):
+            self.tell(self.far_free.at[part, sub], (p.far, p.fsdp))
+
+    def add_jump(self):
+        p = self.place
+        self.copy_jump().wait_recv()
+        self.add_column(p.z, self.slots.near.at[0])
+        for sub in range(SUBS // 2, SUBS):
+            self.tell(self.near_free.at[sub], (p.near, p.fsdp))
+        self.copy_axis(0).start()
+        self.copy_axis(1).start()
+
+    def add_far_axis(self):
+        p = self.place
+        for part in range(2):
+            self.copy_axis(part).wait_recv()
+            self.add_block(p.dp if part else p.near, part)
+        self.copy_axis(2).start()
+
+    def finish(self, out):
+        p = self.place
+        self.copy_axis(2).wait_recv()
+
+        def one(index, _):
+            start = pl.multiple_of(index * self.tile, self.tile)
+            at = pl.ds(pl.multiple_of(self.first + start, self.tile), self.tile)
+            total = self.whole[p.dp, p.z, p.core, at, :].astype(jnp.float32)
+            out[pl.ds(start, self.tile), :] = total + self.slots.along[0, 2, at, :].astype(jnp.float32)
+            return 0
+
+        lax.fori_loop(0, self.count // self.tile, one, 0)
+        for sub in range(SUBS // 2, SUBS):
+            for step in range(1, p.depth):
+                self.tell(self.z_free.at[sub, step - 1], p.along(p.down(step)))
+
+    def drain(self):
+        for at in range(4):
+            self.copy_core(at).wait_send()
+        for part in range(2):
+            self.copy_pair(part).wait_send()
+        self.copy_jump().wait_send()
+        for part in range(3):
+            self.copy_axis(part).wait_send()
 
 
 def outer_gradient(acts, low, grads, row):
@@ -830,6 +1049,18 @@
         table[dp, z, core, 8:9, :] = bias_sum[:, index * 128 : (index + 1) * 128]
 
 
+EARLY = 2
+SCHEDULE = (
+    ("outer",), ("hidden",), ("far", 0), ("inner",), ("far", 1), ("line", 0), ("near", 0), ("total",), ("line", 1),
+    ("go", 4), ("far", 2), ("near", 1), ("norm",), ("go", 5), ("attn",), ("context",), ("far", 3), ("go", 6),
+    ("near", 2), ("heads", 0), ("heads", 1), ("line", 2), ("merged",), ("go", 7), ("far", 4), ("near", 3), ("end", 0),
+    ("far", 5), ("go", 8), ("near", 4), ("end", 1), ("line", 3), ("pack",), ("states",), ("far", 6), ("go", 9),
+    ("near", 5), ("line", 4), ("end", 2), ("go", 10), ("far", 7), ("near", 6), ("end", 3), ("far", 8), ("near", 7),
+    ("end", 4), ("far", 9), ("near", 8), ("end", 5), ("far", 10), ("near", 9), ("end", 6), ("near", 10), ("end", 7),
+    ("end", 8), ("end", 9), ("end", 10),
+)
+
+
 def backward_kernel(depth, block, *refs):
     (vectors, known, rows_in, activated_in, slope_in, outer_low_in, second_grad_in, first_sum_in, first_low_in, context_in,
      projected_in, probs_in, merged_in, attn_in, inner_in, outer_in) = refs[:16]
@@ -875,8 +1106,9 @@
     table_slots = Slots(table_core, table_far, table_near, table_z)
     outers = [
         Scatter(place, outer_grads, slots, sems, credits, sub, 0, sub * lines, lines, before=True, late_before=True)
-        for sub in range(SUBS)
+        for sub in range(SUBS // 2)
     ]
+    line = ScatterLine(place, outer_grads, slots, sems, credits, SUBS - 1, 0, SUBS // 2 * lines, SUBS // 2 * lines)
     inner_grads = first_buffer
     inners = [
         Scatter(place, inner_grads, slots, sems, credits, SUBS + sub, 1, sub * lines, lines, after=True, before=True)
@@ -887,8 +1119,8 @@
         Scatter(place, other_grads, slots, sems, credits, 2 * SUBS + sub, 0, sub * lines, lines, after=True, late_after=True)
         for sub in range(SUBS)
     ]
-    attn_net = others[3]
-    mergeds = others[:3]
+    attn_net = others[0]
+    mergeds = others[1:]
     small = Scatter(place, table, table_slots, sems, credits, 3 * SUBS, 0, 0, 16)
     row_order = (place.both, place.near, place.far, place.dp)
     sums[...] = known[...]
@@ -912,28 +1144,26 @@
         added(3)
 
     order = outers + inners + [attn_net] + mergeds + [small]
-    outs = [outer_out.at[pl.ds(sub * lines, lines), :] for sub in range(SUBS)]
+    outs = [outer_out.at[pl.ds(sub * lines, lines), :] for sub in range(SUBS // 2)]
     outs += [inner_out.at[:, pl.ds(sub * width, width)] for sub in range(SUBS)]
     outs += [attn_out, query_out, key_out, value_out, table_out]
-    window = 3
-
-    def pump(number):
-        if number < len(order):
-            order[number].add_far(1)
-            order[number].add_far(0)
-        if number + window < len(order):
-            order[number + window].start_far(1)
-            order[number + window].start_far(0)
-        if 1 <= number <= len(order):
-            order[number - 1].add_near()
-        if 3 <= number:
-            order[number - 3].finish(outs[number - 3])
-
-    low_load.wait()
-    for copy in act_loads:
-        copy.wait()
-    pieces(outers, lambda row: outer_gradient(wide, low, outer_grads, row), outers[:window])
-    attn_loads = [load(attn_in.at[part * tokens : (part + 1) * tokens], wide.at[part]) for part in range(2)]
+    def far(number):
+        order[number].add_far(1)
+        order[number].add_far(0)
+
+    def go(number):
+        order[number].start_far(1)
+        order[number].start_far(0)
+
+    def near(number):
+        order[number].add_near()
+
+    def end(number):
+        order[number].finish(outs[number])
+
+    def ready(copies):
+        for copy in copies:
+            copy.wait()
 
     def load_merged(part):
         return [
@@ -941,60 +1171,84 @@
             for at in range(2)
         ]
 
-    merged_loads = load_merged(0)
-    outer_load.wait()
-    for copy in slope_loads:
-        copy.wait()
-    for part in range(SUBS):
-        hidden_back(low, first_buffer, wide, bias_sum, part)
-    first_low_load.wait()
-
-    def inner_rows(row):
+    late_loads = []
+
+    def outer_step():
+        ready([low_load] + act_loads)
+        pieces(outers + [line], lambda row: outer_gradient(wide, low, outer_grads, row), outers)
+        line.start_pair()
+        late_loads.append(load(attn_in.at[:tokens], wide.at[0]))
+        late_loads.append(load(attn_in.at[tokens:], wide.at[1]))
+        late_loads.extend(load_merged(0))
+
+    def hidden_step():
+        ready([outer_load] + slope_loads)
         for part in range(SUBS):
-            input_gradient(first_low, wide[SUBS + part], inner_grads, row, part)
-
-    pump(0)
-    pieces(inners, inner_rows)
-    pump(1)
-    grad_load.wait()
-    for copy in inner_loads:
-        copy.wait()
-    first_total_rows(grad, wide, second_buffer)
-    merged_loads += load_merged(1) + load_merged(2)
-    first_sum_load.wait()
-    first_back(first_sum, grad, low, vectors, sums)
-    pump(2)
-    context_load.wait()
-    pieces([attn_net], lambda row: input_gradient(context, low[...], other_grads, row, 3))
-    for copy in attn_loads:
-        copy.wait()
-    context_back(low, wide, context)
-    projected_load.wait()
-    probs_load.wait()
-    pump(3)
-    count = probs.shape[0]
-    attend_back(projected, probs, context, sums, 0, count // 2)
-    pump(4)
-    attend_back(projected, probs, context, sums, count // 2, count)
-    rows_load.wait()
-
-    def merged_rows(row):
-        for part in range(3):
-            input_gradient(rows, projected[:, part * width : (part + 1) * width], other_grads, row, part)
-
-    pieces(mergeds, merged_rows)
-    pump(5)
-    pack_sums(sums, bias_sum, block, table)
-    pieces([small], lambda row: None)
-    pump(6)
-    for copy in merged_loads:
-        copy.wait()
-    states_back(grad, projected, wide)
+            hidden_back(low, first_buffer, wide, bias_sum, part)
+
+    def inner_step():
+        def compute(row):
+            for part in range(SUBS):
+                input_gradient(first_low, wide[SUBS + part], inner_grads, row, part)
+
+        ready([first_low_load])
+        pieces(inners, compute, inners[:EARLY])
+
+    def total_step():
+        ready([grad_load] + inner_loads)
+        first_total_rows(grad, wide, second_buffer)
+        late_loads.extend(load_merged(1) + load_merged(2))
+
+    def norm_step():
+        ready([first_sum_load])
+        first_back(first_sum, grad, low, vectors, sums)
+
+    def attn_step():
+        ready([context_load])
+        pieces([attn_net], lambda row: input_gradient(context, low[...], other_grads, row, 0))
+
+    def context_step():
+        ready(late_loads[:2])
+        context_back(low, wide, context)
+
+    def heads_step(part):
+        if part == 0:
+            ready([projected_load, probs_load])
+        count = probs.shape[0]
+        attend_back(projected, probs, context, sums, part * count // 2, (part + 1) * count // 2)
+
+    def merged_step():
+        def compute(row):
+            for part in range(3):
+                input_gradient(rows, projected[:, part * width : (part + 1) * width], other_grads, row, 1 + part)
+
+        ready([rows_load])
+        pieces(mergeds, compute)
+
+    def pack_step():
+        pack_sums(sums, bias_sum, block, table)
+        pieces([small], lambda row: None)
+
     save = pltpu.make_async_copy(grad, states_out, save_sem)
-    save.start()
-    for number in range(7, len(order) + 3):
-        pump(number)
-    for net in order:
+
+    def states_step():
+        ready(late_loads[2:])
+        states_back(grad, projected, wide)
+        save.start()
+
+    def line_step(part):
+        (line.add_pair, line.add_jump, line.add_far_axis, line.finish)[max(part - 1, 0)](
+            *(((1,), (0,), (), (), (outer_out.at[pl.ds(SUBS // 2 * lines, SUBS // 2 * lines), :],))[part])
+        )
+
+    steps = {
+        "outer": outer_step, "hidden": hidden_step, "inner": inner_step, "total": total_step, "norm": norm_step,
+        "attn": attn_step, "context": context_step, "heads": heads_step, "merged": merged_step, "pack": pack_step,
+        "states": states_step, "line": line_step, "go": go, "far": far, "near": near, "end": end,
+    }
+    for entry in SCHEDULE:
+        steps[entry[0]](*entry[1:])
+    for net in order + [line]:
         net.drain()
     save.wait()
 
@@ -1055,6 +1309,43 @@
     )(vectors, known, *kept)
 
 
+def finish_kernel(block, *refs):
+    count = 8
+    table = refs[0]
+    sources, targets = refs[1 : 1 + count], refs[1 + count : 1 + 2 * count]
+    rows = refs[1 + 2 * count : 10 + 2 * count]
+    held = refs[10 + 2 * count : 10 + 3 * count]
+    in_sem, out_sem = refs[10 + 3 * count :]
+    fetches = [pltpu.make_async_copy(source, target, in_sem.at[at]) for at, (source, target) in enumerate(zip(sources, held))]
+    stores = [pltpu.make_async_copy(source, target, out_sem.at[at]) for at, (source, target) in enumerate(zip(held, targets))]
+    for copy in fetches:
+        copy.start()
+    for index, row in enumerate(rows):
+        row[...] = table[index, : row.shape[0]]
+    for fetch, store in zip(fetches, stores):
+        fetch.wait()
+        store.start()
+    for store in stores:
+        store.wait()
+
+
+def finish_all(block, table, arrays):
+    shapes = [jax.ShapeDtypeStruct(array.shape, array.dtype) for array in arrays]
+    shapes += [jax.ShapeDtypeStruct((block,), jnp.float32)] * 8 + [jax.ShapeDtypeStruct((128,), jnp.float32)]
+    here = pl.BlockSpec(memory_space=pltpu.VMEM)
+    away = pl.BlockSpec(memory_space=pltpu.HBM)
+    dma = pltpu.SemaphoreType.DMA
+    return pl.pallas_call(
+        functools.partial(finish_kernel, block),
+        out_shape=shapes,
+        in_specs=[here] + [away] * len(arrays),
+        out_specs=[away] * len(arrays) + [here] * 9,
+        scratch_shapes=[pltpu.VMEM(array.shape, array.dtype) for array in arrays] + [dma((len(arrays),))] * 2,
+        compiler_params=pltpu.CompilerParams(vmem_limit_bytes=60 * 1024 * 1024),
+        name="finish",
+    )(table, *arrays)
+
+
 def normalize(hidden, gain, shift):
     center = hidden - jnp.mean(hidden, axis=-1, keepdims=True)
     spread = jnp.mean(center * center, axis=-1, keepdims=True)
@@ -1224,15 +1515,6 @@
     )
 
 
-def pack_vectors(vectors):
-    row = lax.broadcasted_iota(jnp.int32, (16, 128), 0)
-    table = jnp.zeros((16, 128), jnp.float32)
-    for index, vector in enumerate(vectors):
-        padded = jnp.pad(vector.astype(jnp.float32), (0, 128 - vector.shape[0]))
-        table = jnp.where(row == index, padded[None, :], table)
-    return table
-
-
 def shards(depth, *arrays):
     (states, pad_mask, query_proj, key_proj, value_proj, attn_proj, query_bias, value_bias, attn_bias, first_gain,
      first_shift, inner_proj, inner_bias, outer_proj, outer_bias, second_gain, second_shift, out_grad) = arrays
@@ -1260,19 +1542,18 @@
                   outer_proj, out_grad):
     width = states.shape[1]
     block = short[0].shape[0]
-    packed = pack_vectors(short + (inner_bias,))
     (merged, attn, inner, outer, encoded, projected, probs, context, first_sum, first_low, activated, slope, second_grad,
      outer_low, vectors, sums) = forward_all(
         depth, block, states, pad_mask, out_grad,
-        (query_proj, key_proj, value_proj, attn_proj, inner_proj, outer_proj, packed))
+        (query_proj, key_proj, value_proj, attn_proj, inner_proj, outer_proj, *short, inner_bias))
     states_part, outer_sum, inner_sum, query_sum, key_sum, value_sum, attn_sum, table_sum = backward_all(
         depth, block, vectors, sums,
         (states, activated, slope, outer_low, second_grad, first_sum, first_low, context, projected, probs,
          merged.reshape(width, -1), attn.reshape(width, -1), inner, outer))
-    short_sums = [table_sum[index, :block] for index in range(8)]
-    widened_sum = table_sum[8, : inner_bias.shape[0]]
-    return (encoded, states_part, query_sum, key_sum, value_sum, attn_sum, *short_sums[:5], inner_sum, widened_sum,
-            outer_sum, *short_sums[5:])
+    (encoded, states_part, query_sum, key_sum, value_sum, attn_sum, inner_sum, outer_sum, *rows) = finish_all(
+        block, table_sum, (encoded, states_part, query_sum, key_sum, value_sum, attn_sum, inner_sum, outer_sum))
+    return (encoded, states_part, query_sum, key_sum, value_sum, attn_sum, *rows[:5], inner_sum, rows[8], outer_sum,
+            *rows[5:8])
 
 
 def solution(mesh):
@@ -1283,7 +1564,7 @@
     def whole(*arrays):
         rows = arrays[2].shape[0] // (dps * others)
         tiles = rows % 16 == 0 and arrays[12].shape[0] == 128 * dps * others
-        depth = others // 2 if tiles and dps == 4 and others % 2 == 0 else 0
+        depth = others // 2 if tiles and dps == 4 and others == 2 * dps else 0
         return jax.shard_map(
             functools.partial(shards, depth),
             mesh=mesh,

time: 272 us -> 256 us (0.941)
  local copies, waits for them, and re-layouts: 9.38 us -> 0 us
  other arithmetic: 4.08 us -> 0 us
    unnamed x24 -> x0, local copies, waits for them, and re-layouts: 6.53 us -> none
    pallas_call x1, Pallas kernels: 130 us -> 124 us  [forward_all(): pl.pallas_call(functools.partial(forward_kernel, depth, block), out_shape...]
    pallas_call x0 -> x1, Pallas kernels: none -> 5.15 us  [finish_all(): pl.pallas_call(functools.partial(finish_kernel, block), out_shape=shapes,...]
    squeeze x2 -> x0, local copies, waits for them, and re-layouts: 2.85 us -> none  [the longest x1 1.52 us: kernel_shards(): short_sums = [table_sum[index, :block] for index in range(8)]]
where the time goes in v2:
time: 256 us
  Pallas kernels  255 us (100%)
    pallas_call x1, Pallas kernels, backward_all(): pl.pallas_call(functools.partial(backward_kernel, depth, block), out_shap...  126 us
    pallas_call x1, Pallas kernels, forward_all(): pl.pallas_call(functools.partial(forward_kernel, depth, block), out_shape...  124 us
    pallas_call x1, Pallas kernels, finish_all(): pl.pallas_call(functools.partial(finish_kernel, block), out_shape=shapes,...  5.15 us

profile of v2, /device:TPU:0, one launch (start us, length us, event | category | flops | bytes accessed | tf_op | source)
XLA Modules:
  0.0 256.0 jit_solution(1160795837216804208)
XLA Ops:
  0.7 124.0 %forward.1 = (bf16[4,4,2,32,3072]{4,3,2,1,0:T(8,128)(2,1)}, bf16[4,4,2,32,1024]{4,3,2,1,0:T(8,128)(2,1)}, bf16[4,4,2,32,4096]{4,3,2,1,0:T(8,128)(2,1)}, bf16[4,4...) custom-call(bf16[512,1024]{1,0:T(8,128)(2,1)} %refs_2_.3, ...), custom_call_target="tpu_custom_call" | custom-call | tf_op jit(solution)/shard_map/forward/pallas_call | solution.py:630
  124.6 126.0 %backward.1 = (f32[512,1024]{1,0:T(8,128)}, f32[128,1024]{1,0:T(8,128)}, f32[32,4096]{1,0:T(8,128)}, f32[32,1024]{1,0:T(8,128)}, f32[32,1024]{1,0:T(8,128)}, /*i...) custom-call(f32[8,1024]{1,0:T(8,128)} %get-tuple-element.58.refs_0_, f32[8,1024]{1,0:T(8,128)} %get-tuple-element.59.refs_1_, ...), custom_call_target="tpu_custom_call" | custom-call | tf_op jit(solution)/shard_map/backward/pallas_call | solution.py:1299
  250.7 5.1 %finish.1 = (bf16[512,1024]{1,0:T(8,128)(2,1)}, f32[512,1024]{1,0:T(8,128)}, f32[32,1024]{1,0:T(8,128)}, f32[32,1024]{1,0:T(8,128)}, f32[32,1024]{1,0:T(8,128)},...) custom-call(f32[16,128]{1,0:T(8,128)} %get-tuple-element.73.refs_0_,, ...), custom_call_target="tpu_custom_call" | custom-call | tf_op jit(solution)/shard_map/finish/pallas_call | solution.py:1338

commit v3 on v2

--- a/solution.py
+++ b/solution.py
@@ -48,7 +48,9 @@
         others += [(self.near, self.fsdp), (self.far, self.fsdp), (self.dp, self.sibling)]
         for other in others:
             pl.semaphore_signal(barrier, inc=1, device_id=other, device_id_type=MESH)
-        pl.semaphore_wait(barrier, len(others))
+
+    def greeted(self):
+        pl.semaphore_wait(pltpu.get_barrier_semaphore(), self.depth + 2)
 
 
 def remote(source, target, send, recv, device):
@@ -430,8 +432,7 @@
     return rate * (scaled - mean - normed * along)
 
 
-def second_block(first_norm, total, cotangent, vectors, encoded, second_grad, outer_low, sums):
-    sums[...] = jnp.zeros_like(sums)
+def second_block(first_norm, total, cotangent, vectors, encoded, second_grad, outer_low, sums, first, last):
 
     def one(index, _):
         at = span(index, 64)
@@ -448,22 +449,27 @@
         sums[7:8, :] += jnp.sum(grad, axis=0, keepdims=True)
         return 0
 
-    lax.fori_loop(0, first_norm.shape[0] // 64, one, 0)
+    lax.fori_loop(first, last, one, 0)
 
 
 def forward_kernel(depth, block, *refs):
-    (rows, keep, cotangent, query_own, key_own, value_own, attn_own, inner_own, outer_own) = refs[:9]
+    (rows_in, keep, cotangent_in, query_own, key_own, value_own, attn_own, inner_own, outer_own) = refs[:9]
     short_vectors = refs[9:18]
     merged_out, attn_out, inner_out, outer_out = refs[18:22]
     (encoded_out, projected_out, probs_out, context_out, first_sum_out, first_low_out, activated_out, slope_out,
      second_grad_out, outer_low_out, vectors, sums) = refs[22:34]
     (table_own, merged_own, table, merged, attn, inner, outer, projected, probs, context, first_sum, first_norm, first_low,
-     activated, slope, total, encoded, second_grad, outer_low, long_bias, save_sem) = refs[34:55]
-    sems = refs[55:]
+     activated, slope, total, encoded, second_grad, outer_low, long_bias, save_sem, rows, cotangent, load_sem) = refs[34:58]
+    sems = refs[58:]
+    place = Place(depth)
+    place.greet()
+    loads = [
+        pltpu.make_async_copy(rows_in, rows, load_sem.at[0]),
+        pltpu.make_async_copy(cotangent_in, cotangent, load_sem.at[1]),
+    ]
     table_own[...] = jnp.zeros_like(table_own)
     for index, vector in enumerate(short_vectors):
         table_own[index, : vector.shape[0]] = vector[...].astype(jnp.float32)
-    place = Place(depth)
     width = rows.shape[1]
     for part, own in enumerate((query_own, key_own, value_own)):
         merged_own[:, part * width : (part + 1) * width] = own[...]
@@ -476,7 +482,9 @@
     line = GatherLine(place, outer, outer_own, sems, 5, pl.ds(half, half))
     nets = (net_table, net_merged, net_attn, net_inner, net_outer, line)
     front = nets[:3]
-    place.greet()
+    place.greeted()
+    for copy in loads:
+        copy.start()
     saves = []
 
     def save(source, target):
@@ -525,6 +533,7 @@
     save(merged, merged_out)
     save(attn, attn_out)
     unpack_table(table, block, vectors, long_bias)
+    loads[0].wait()
     project(rows, merged, vectors, projected)
     save(projected, projected_out)
     for step in range(2, depth - 1):
@@ -565,6 +574,8 @@
     inner_quarter(3)
     save(activated, activated_out)
     save(slope, slope_out)
+    sums[...] = jnp.zeros_like(sums)
+    loads[1].wait()
     line.arrive_core()
     net_outer.arrive_core(0)
     outer_part(activated, outer, place.dp, total, True)
@@ -576,10 +587,16 @@
     net_outer.arrive_core(3)
     save(outer, outer_out)
     outer_part(activated, outer, place.both, total, False)
-    second_block(first_norm, total, cotangent, vectors, encoded, second_grad, outer_low, sums)
-    save(encoded, encoded_out)
-    save(second_grad, second_grad_out)
-    save(outer_low, outer_low_out)
+    for part in range(4):
+        size = rows.shape[0] // 4
+        second_block(
+            first_norm, total, cotangent, vectors, encoded, second_grad, outer_low, sums, part * size // 64,
+            (part + 1) * size // 64,
+        )
+        at = pl.ds(part * size, size)
+        save(outer_low.at[at], outer_low_out.at[at])
+        save(second_grad.at[at], second_grad_out.at[at])
+        save(encoded.at[at], encoded_out.at[at])
     for net in nets:
         net.drain()
     for copy in saves:
@@ -624,13 +641,14 @@
     scratch += [pltpu.VMEM((tokens, width), high)]
     scratch += [held[name] for name in ("encoded", "second_grad", "outer_low")]
     scratch += [pltpu.VMEM((1, hidden), high)]
-    scratch += [pltpu.SemaphoreType.DMA((len(full_shapes) + len(kept),))]
+    scratch += [pltpu.SemaphoreType.DMA((len(full_shapes) + len(kept) + 9,))]
+    scratch += [pltpu.VMEM((tokens, width), low), pltpu.VMEM((tokens, width), low), pltpu.SemaphoreType.DMA((2,))]
     here = pl.BlockSpec(memory_space=pltpu.VMEM)
     away = pl.BlockSpec(memory_space=pl.ANY)
     return pl.pallas_call(
         functools.partial(forward_kernel, depth, block),
         out_shape=shapes,
-        in_specs=[here] * (3 + len(owns)),
+        in_specs=[away, here, away] + [here] * len(owns),
         out_specs=[away] * (len(full_shapes) + len(kept)) + [here] * 2,
         scratch_shapes=scratch + gather_sems(6, depth),
         compiler_params=pltpu.CompilerParams(
@@ -655,7 +673,7 @@
         self.sc, self.rc, self.sa, self.ra, self.sb, self.rb, self.sz, self.rz = sems
         self.core_free, self.far_free, self.near_free, self.z_free = credits
         self.number, self.lot, self.first, self.count = number, lot, first, count
-        self.sub = first // count
+        self.sub = first * SUBS // whole.shape[3]
         self.after, self.before, self.late_after, self.late_before = after, before, late_after, late_before
         self.tile = 8 if whole.dtype == jnp.float32 else 16
 
@@ -1052,12 +1070,12 @@
 EARLY = 2
 SCHEDULE = (
     ("outer",), ("hidden",), ("far", 0), ("inner",), ("far", 1), ("line", 0), ("near", 0), ("total",), ("line", 1),
-    ("go", 4), ("far", 2), ("near", 1), ("norm",), ("go", 5), ("attn",), ("context",), ("far", 3), ("go", 6),
-    ("near", 2), ("heads", 0), ("heads", 1), ("line", 2), ("merged",), ("go", 7), ("far", 4), ("near", 3), ("end", 0),
+    ("go", 4), ("norm",), ("attn",), ("go", 6), ("context",), ("far", 2), ("near", 1), ("heads", 0), ("go", 5),
+    ("heads", 1), ("far", 3), ("near", 2), ("line", 2), ("merged",), ("go", 7), ("far", 4), ("near", 3), ("end", 0),
     ("far", 5), ("go", 8), ("near", 4), ("end", 1), ("line", 3), ("pack",), ("states",), ("far", 6), ("go", 9),
-    ("near", 5), ("line", 4), ("end", 2), ("go", 10), ("far", 7), ("near", 6), ("end", 3), ("far", 8), ("near", 7),
-    ("end", 4), ("far", 9), ("near", 8), ("end", 5), ("far", 10), ("near", 9), ("end", 6), ("near", 10), ("end", 7),
-    ("end", 8), ("end", 9), ("end", 10),
+    ("go", 10), ("near", 5), ("line", 4), ("end", 2), ("far", 7), ("go", 11), ("near", 6), ("end", 3), ("far", 8),
+    ("near", 7), ("end", 4), ("far", 9), ("far", 10), ("near", 8), ("end", 5), ("near", 9), ("far", 11), ("near", 10),
+    ("end", 6), ("end", 7), ("near", 11), ("end", 8), ("end", 9), ("end", 10), ("end", 11),
 )
 
 
@@ -1071,6 +1089,7 @@
     sems = refs[49:57]
     credits = refs[57:61]
     place = Place(depth)
+    place.greet()
     width = rows.shape[1]
     tokens = rows.shape[0]
     lines = outer_grads.shape[3] // SUBS
@@ -1117,17 +1136,21 @@
     other_grads = second_buffer
     others = [
         Scatter(place, other_grads, slots, sems, credits, 2 * SUBS + sub, 0, sub * lines, lines, after=True, late_after=True)
-        for sub in range(SUBS)
+        for sub in range(SUBS - 1)
     ]
     attn_net = others[0]
-    mergeds = others[1:]
+    mergeds = others[1:3]
+    lowest = lines // 2
+    mergeds += [
+        Scatter(place, other_grads, slots, sems, credits, 3 * SUBS - 1, 0, 3 * lines, lowest, after=True, late_after=True),
+        Scatter(place, other_grads, slots, sems, credits, 3 * SUBS + 1, 0, 3 * lines + lowest, lowest),
+    ]
     small = Scatter(place, table, table_slots, sems, credits, 3 * SUBS, 0, 0, 16)
     row_order = (place.both, place.near, place.far, place.dp)
     sums[...] = known[...]
     sums[0:2, :] = jnp.zeros((2, width), jnp.float32)
-    place.greet()
-
-    def pieces(nets, compute, early=()):
+
+    def pieces(nets, compute, early=(), first=False):
         def added(at):
             for net in nets:
                 net.add_core(at)
@@ -1137,16 +1160,18 @@
 
         for at in range(4):
             compute(row_order[at])
+            if first and at == 0:
+                place.greeted()
             for net in nets:
                 net.start_core(at)
             if at:
                 added(at - 1)
         added(3)
 
-    order = outers + inners + [attn_net] + mergeds + [small]
+    order = outers + inners + [attn_net] + mergeds[:2] + [small] + mergeds[2:]
     outs = [outer_out.at[pl.ds(sub * lines, lines), :] for sub in range(SUBS // 2)]
     outs += [inner_out.at[:, pl.ds(sub * width, width)] for sub in range(SUBS)]
-    outs += [attn_out, query_out, key_out, value_out, table_out]
+    outs += [attn_out, query_out, key_out, table_out, value_out.at[pl.ds(0, lowest), :], value_out.at[pl.ds(lowest, lowest), :]]
     def far(number):
         order[number].add_far(1)
         order[number].add_far(0)
@@ -1175,7 +1200,7 @@
 
     def outer_step():
         ready([low_load] + act_loads)
-        pieces(outers + [line], lambda row: outer_gradient(wide, low, outer_grads, row), outers)
+        pieces(outers + [line], lambda row: outer_gradient(wide, low, outer_grads, row), outers, True)
         line.start_pair()
         late_loads.append(load(attn_in.at[:tokens], wide.at[0]))
         late_loads.append(load(attn_in.at[tokens:], wide.at[1]))
@@ -1262,7 +1287,7 @@
     lines = unit[3]
     own_rows = lines // SUBS
     dma, regular = pltpu.SemaphoreType.DMA, pltpu.SemaphoreType.REGULAR
-    nets = 3 * SUBS + 1
+    nets = 3 * SUBS + 2
     scratch = [
         pltpu.VMEM(unit, low),
         pltpu.VMEM(unit, low),

time: 256 us -> 251 us (0.980)
  Pallas kernels: 255 us -> 250 us
    pallas_call x1, Pallas kernels: 126 us -> 122 us  [backward_all(): pl.pallas_call(functools.partial(backward_kernel, depth, block), out_shap...]
where the time goes in v3:
time: 251 us
  Pallas kernels  250 us (100%)
    pallas_call x1, Pallas kernels, forward_all(): pl.pallas_call(functools.partial(forward_kernel, depth, block), out_shape...  122 us
    pallas_call x1, Pallas kernels, backward_all(): pl.pallas_call(functools.partial(backward_kernel, depth, block), out_shap...  122 us
    pallas_call x1, Pallas kernels, finish_all(): pl.pallas_call(functools.partial(finish_kernel, block), out_shape=shapes,...  5.15 us

profile of v3, /device:TPU:0, one launch (start us, length us, event | category | flops | bytes accessed | tf_op | source)
XLA Modules:
  0.0 250.7 jit_solution(18162913028733398763)
XLA Ops:
  0.7 122.5 %forward.1 = (bf16[4,4,2,32,3072]{4,3,2,1,0:T(8,128)(2,1)}, bf16[4,4,2,32,1024]{4,3,2,1,0:T(8,128)(2,1)}, bf16[4,4,2,32,4096]{4,3,2,1,0:T(8,128)(2,1)}, bf16[4,4...) custom-call(bf16[512,1024]{1,0:T(8,128)(2,1)} %refs_2_.3, ...), custom_call_target="tpu_custom_call" | custom-call | tf_op jit(solution)/shard_map/forward/pallas_call | solution.py:648
  123.1 122.2 %backward.1 = (f32[512,1024]{1,0:T(8,128)}, f32[128,1024]{1,0:T(8,128)}, f32[32,4096]{1,0:T(8,128)}, f32[32,1024]{1,0:T(8,128)}, f32[32,1024]{1,0:T(8,128)}, /*i...) custom-call(f32[8,1024]{1,0:T(8,128)} %get-tuple-element.58.refs_0_, f32[8,1024]{1,0:T(8,128)} %get-tuple-element.59.refs_1_, ...), custom_call_target="tpu_custom_call" | custom-call | tf_op jit(solution)/shard_map/backward/pallas_call | solution.py:1324
  245.3 5.1 %finish.1 = (bf16[512,1024]{1,0:T(8,128)(2,1)}, f32[512,1024]{1,0:T(8,128)}, f32[32,1024]{1,0:T(8,128)}, f32[32,1024]{1,0:T(8,128)}, f32[32,1024]{1,0:T(8,128)},...) custom-call(f32[16,128]{1,0:T(8,128)} %get-tuple-element.73.refs_0_,, ...), custom_call_target="tpu_custom_call" | custom-call | tf_op jit(solution)/shard_map/finish/pallas_call | solution.py:1363

commit v4 on v3

--- a/solution.py
+++ b/solution.py
@@ -541,10 +541,10 @@
     net_inner.last_hop()
     net_inner.send(depth - 1)
     net_inner.spread(depth - 2)
-    line.relay()
     count = probs.shape[0]
     attend(projected, keep, probs, context, 0, count // 2)
     net_outer.last_hop()
+    line.relay()
     net_inner.spread(depth - 1)
     attend(projected, keep, probs, context, count // 2, count)
     save(probs, probs_out)
@@ -1067,15 +1067,15 @@
         table[dp, z, core, 8:9, :] = bias_sum[:, index * 128 : (index + 1) * 128]
 
 
-EARLY = 2
+EARLY = 3
 SCHEDULE = (
-    ("outer",), ("hidden",), ("far", 0), ("inner",), ("far", 1), ("line", 0), ("near", 0), ("total",), ("line", 1),
-    ("go", 4), ("norm",), ("attn",), ("go", 6), ("context",), ("far", 2), ("near", 1), ("heads", 0), ("go", 5),
-    ("heads", 1), ("far", 3), ("near", 2), ("line", 2), ("merged",), ("go", 7), ("far", 4), ("near", 3), ("end", 0),
-    ("far", 5), ("go", 8), ("near", 4), ("end", 1), ("line", 3), ("pack",), ("states",), ("far", 6), ("go", 9),
-    ("go", 10), ("near", 5), ("line", 4), ("end", 2), ("far", 7), ("go", 11), ("near", 6), ("end", 3), ("far", 8),
-    ("near", 7), ("end", 4), ("far", 9), ("far", 10), ("near", 8), ("end", 5), ("near", 9), ("far", 11), ("near", 10),
-    ("end", 6), ("end", 7), ("near", 11), ("end", 8), ("end", 9), ("end", 10), ("end", 11),
+    ("outer",), ("hidden",), ("far", 0), ("inner",), ("line", 0), ("far", 1), ("near", 0), ("total",), ("line", 1),
+    ("norm",), ("attn",), ("context",), ("far", 2), ("go", 5), ("go", 6), ("near", 1), ("heads", 0), ("heads", 1),
+    ("far", 3), ("near", 2), ("line", 2), ("merged",), ("go", 7), ("far", 4), ("near", 3), ("end", 0), ("far", 5),
+    ("go", 8), ("near", 4), ("end", 1), ("line", 3), ("pack",), ("states",), ("far", 6), ("go", 9), ("go", 10),
+    ("near", 5), ("line", 4), ("end", 2), ("far", 7), ("go", 11), ("near", 6), ("end", 3), ("far", 8), ("near", 7),
+    ("end", 4), ("far", 9), ("far", 10), ("near", 8), ("end", 5), ("near", 9), ("far", 11), ("near", 10), ("end", 6),
+    ("end", 7), ("near", 11), ("end", 8), ("end", 9), ("end", 10), ("end", 11),
 )
 
 

time: 251 us -> 251 us (level)
  no operation moved by 1% of the time
where the time goes in v4:
time: 251 us
  Pallas kernels  250 us (100%)
    pallas_call x1, Pallas kernels, backward_all(): pl.pallas_call(functools.partial(backward_kernel, depth, block), out_shap...  123 us
    pallas_call x1, Pallas kernels, forward_all(): pl.pallas_call(functools.partial(forward_kernel, depth, block), out_shape...  122 us
    pallas_call x1, Pallas kernels, finish_all(): pl.pallas_call(functools.partial(finish_kernel, block), out_shape=shapes,...  5.15 us

profile of v4, /device:TPU:0, one launch (start us, length us, event | category | flops | bytes accessed | tf_op | source)
XLA Modules:
  0.0 251.0 jit_solution(14147097521484974791)
XLA Ops:
  0.7 122.5 %forward.1 = (bf16[4,4,2,32,3072]{4,3,2,1,0:T(8,128)(2,1)}, bf16[4,4,2,32,1024]{4,3,2,1,0:T(8,128)(2,1)}, bf16[4,4,2,32,4096]{4,3,2,1,0:T(8,128)(2,1)}, bf16[4,4...) custom-call(bf16[512,1024]{1,0:T(8,128)(2,1)} %refs_2_.3, ...), custom_call_target="tpu_custom_call" | custom-call | tf_op jit(solution)/shard_map/forward/pallas_call | solution.py:648
  123.1 122.5 %backward.1 = (f32[512,1024]{1,0:T(8,128)}, f32[128,1024]{1,0:T(8,128)}, f32[32,4096]{1,0:T(8,128)}, f32[32,1024]{1,0:T(8,128)}, f32[32,1024]{1,0:T(8,128)}, /*i...) custom-call(f32[8,1024]{1,0:T(8,128)} %get-tuple-element.58.refs_0_, f32[8,1024]{1,0:T(8,128)} %get-tuple-element.59.refs_1_, ...), custom_call_target="tpu_custom_call" | custom-call | tf_op jit(solution)/shard_map/backward/pallas_call | solution.py:1324
  245.7 5.1 %finish.1 = (bf16[512,1024]{1,0:T(8,128)(2,1)}, f32[512,1024]{1,0:T(8,128)}, f32[32,1024]{1,0:T(8,128)}, f32[32,1024]{1,0:T(8,128)}, f32[32,1024]{1,0:T(8,128)},...) custom-call(f32[16,128]{1,0:T(8,128)} %get-tuple-element.73.refs_0_,, ...), custom_call_target="tpu_custom_call" | custom-call | tf_op jit(solution)/shard_map/finish/pallas_call | solution.py:1363

commit v5 on v3

--- a/solution.py
+++ b/solution.py
@@ -578,14 +578,17 @@
     loads[1].wait()
     line.arrive_core()
     net_outer.arrive_core(0)
+    save(outer.at[place.dp], outer_out.at[place.dp])
     outer_part(activated, outer, place.dp, total, True)
     net_outer.arrive_far(0)
     net_outer.arrive_core(1, 2)
+    for row in (place.near, place.far):
+        save(outer.at[row], outer_out.at[row])
     outer_part(activated, outer, place.near, total, False)
     outer_part(activated, outer, place.far, total, False)
     net_outer.arrive_far(1)
     net_outer.arrive_core(3)
-    save(outer, outer_out)
+    save(outer.at[place.both], outer_out.at[place.both])
     outer_part(activated, outer, place.both, total, False)
     for part in range(4):
         size = rows.shape[0] // 4
@@ -641,7 +644,7 @@
     scratch += [pltpu.VMEM((tokens, width), high)]
     scratch += [held[name] for name in ("encoded", "second_grad", "outer_low")]
     scratch += [pltpu.VMEM((1, hidden), high)]
-    scratch += [pltpu.SemaphoreType.DMA((len(full_shapes) + len(kept) + 9,))]
+    scratch += [pltpu.SemaphoreType.DMA((len(full_shapes) + len(kept) + 12,))]
     scratch += [pltpu.VMEM((tokens, width), low), pltpu.VMEM((tokens, width), low), pltpu.SemaphoreType.DMA((2,))]
     here = pl.BlockSpec(memory_space=pltpu.VMEM)
     away = pl.BlockSpec(memory_space=pl.ANY)

time: 251 us -> 251 us (level)
  no operation moved by 1% of the time
where the time goes in v5:
time: 251 us
  Pallas kernels  250 us (100%)
    pallas_call x1, Pallas kernels, forward_all(): pl.pallas_call(functools.partial(forward_kernel, depth, block), out_shape...  123 us
    pallas_call x1, Pallas kernels, backward_all(): pl.pallas_call(functools.partial(backward_kernel, depth, block), out_shap...  122 us
    pallas_call x1, Pallas kernels, finish_all(): pl.pallas_call(functools.partial(finish_kernel, block), out_shape=shapes,...  5.15 us

profile of v5, /device:TPU:0, one launch (start us, length us, event | category | flops | bytes accessed | tf_op | source)
XLA Modules:
  0.0 250.7 jit_solution(9991985474905755549)
XLA Ops:
  0.7 122.5 %forward.1 = (bf16[4,4,2,32,3072]{4,3,2,1,0:T(8,128)(2,1)}, bf16[4,4,2,32,1024]{4,3,2,1,0:T(8,128)(2,1)}, bf16[4,4,2,32,4096]{4,3,2,1,0:T(8,128)(2,1)}, bf16[4,4...) custom-call(bf16[512,1024]{1,0:T(8,128)(2,1)} %refs_2_.3, ...), custom_call_target="tpu_custom_call" | custom-call | tf_op jit(solution)/shard_map/forward/pallas_call | solution.py:651
  123.2 122.2 %backward.1 = (f32[512,1024]{1,0:T(8,128)}, f32[128,1024]{1,0:T(8,128)}, f32[32,4096]{1,0:T(8,128)}, f32[32,1024]{1,0:T(8,128)}, f32[32,1024]{1,0:T(8,128)}, /*i...) custom-call(f32[8,1024]{1,0:T(8,128)} %get-tuple-element.58.refs_0_, f32[8,1024]{1,0:T(8,128)} %get-tuple-element.59.refs_1_, ...), custom_call_target="tpu_custom_call" | custom-call | tf_op jit(solution)/shard_map/backward/pallas_call | solution.py:1327
  245.4 5.1 %finish.1 = (bf16[512,1024]{1,0:T(8,128)(2,1)}, f32[512,1024]{1,0:T(8,128)}, f32[32,1024]{1,0:T(8,128)}, f32[32,1024]{1,0:T(8,128)}, f32[32,1024]{1,0:T(8,128)},...) custom-call(f32[16,128]{1,0:T(8,128)} %get-tuple-element.73.refs_0_,, ...), custom_call_target="tpu_custom_call" | custom-call | tf_op jit(solution)/shard_map/finish/pallas_call | solution.py:1366
